TPU v7x, 32 devices: a whole 2x2x4 slice. The times are simulated.
32 devices in a mesh: wide: 8 (over z, y), narrow: 4 (over x, core).
Axes of the slice: x: 2, y: 2, z: 4, core: 2. Of those that a mesh axis runs over, the one named last changes fastest.
Arguments:
- parent_front: bfloat16 [3072, 5120], P('wide', 'narrow'), may hold values from -0.078125 to 0.078125
- child_updates: bfloat16 [2048, 2048], P('wide', 'narrow'), may hold values from -0.078125 to 0.078125
- child_map: int32 [2048], P('wide'), may hold values from 0 to 3071, as said below
- tile_mask: int32 [96, 40], P('wide', 'narrow'), may hold values 0 or 1
- probes: bfloat16 [5120, 512], P('narrow'), may hold values from -6 to 6
Outputs:
- probe_image: bfloat16 [3072, 512], P('wide', 'narrow')
Inputs may be any that keep to these rules, and one draw needn't show every extreme that they name: `child_map`: the rows of one child go to distinct parent rows. Of the 256 rows of one child held by one wide device, exactly 32 have parent rows on each wide device w, that is rows w * 384 to (w + 1) * 384 - 1.
All inputs are finite; a program needn't handle non-finite values. No bound on the sum of `tile_mask` on one device may be relied on, other than what follows from the above.
Results may differ from a plain program's by a relative error of at most 0.012.
Values may be sent and summed in bfloat16 or wider, within the bound.
A program may use at most 128 MiB of HBM per device.

v0:
```python
import jax
import jax.numpy as jnp
from jax import lax
from jax.sharding import PartitionSpec as P

TILE = 128


def masked_block(panel_block, mask_part):
    row_count, col_count = panel_block.shape
    tile_view = panel_block.reshape(
        mask_part.shape[0],
        row_count // mask_part.shape[0],
        mask_part.shape[1],
        col_count // mask_part.shape[1],
    )
    return (tile_view * mask_part[:, None, :, None].astype(panel_block.dtype)).reshape(
        row_count, col_count
    )


def local(parent_front, child_updates, child_map, tile_mask, probes):
    rows_dev = parent_front.shape[0]
    touched_cols = child_updates.shape[1]
    wide_count = lax.axis_size("wide")
    per_peer = child_map.shape[0] // wide_count
    split_tiles = touched_cols // TILE
    own_masked = masked_block(parent_front[:, touched_cols:], tile_mask[:, split_tiles:])
    target = child_map // rows_dev
    ordering = jnp.argsort(target, stable=True)
    outgoing = child_updates[ordering].reshape(wide_count, per_peer, touched_cols)
    places = (child_map - target * rows_dev)[ordering].reshape(wide_count, per_peer)
    arrived, arrived_rows = (
        lax.all_to_all(outgoing, "wide", split_axis=0, concat_axis=0, tiled=True),
        lax.all_to_all(places, "wide", split_axis=0, concat_axis=0, tiled=True),
    )
    added_sum = (
        jnp.zeros((rows_dev, touched_cols), jnp.float32)
        .at[arrived_rows.reshape(-1)]
        .add(arrived.reshape(-1, touched_cols).astype(jnp.float32))
    )
    touched = (parent_front[:, :touched_cols].astype(jnp.float32) + added_sum).astype(jnp.bfloat16)
    touched_masked = masked_block(touched, tile_mask[:, :split_tiles])
    masked = jnp.concatenate([touched_masked, own_masked], axis=1)
    partial_value = jnp.dot(masked, probes, preferred_element_type=jnp.float32)
    share_out = lax.psum_scatter(
        partial_value.astype(jnp.bfloat16), "narrow", scatter_dimension=1, tiled=True
    )
    return share_out


def solution(mesh):
    placed = (
        P("wide", "narrow"),
        P("wide", "narrow"),
        P("wide"),
        P("wide", "narrow"),
        P("narrow", None),
    )
    return jax.shard_map(
        local, mesh=mesh, in_specs=placed, out_specs=P("wide", "narrow"), check_vma=False
    )
```

profile of v0, /device:TPU:0, one launch (start us, length us, event | category | flops | bytes accessed | tf_op | source)
XLA Modules:
  0.0 71.3 jit_solution(7282297204626515915)
XLA Ops:
  6.5 0.0 copy-start
  6.5 0.0 copy-start.2
  6.5 0.8 %multiply_subtract_fusion = (s32[256]{0:T(256)S(1)}, s32[256]{0:T(256)S(1)}) fusion(s32[256]{0:T(256)} %param.7), kind=kLoop, calls=%fused_computation.16 | loop fusion | flops 2560 | bytes 3072 | tf_op jit(solution)/shard_map/sub | solution.py:32
  7.4 3.2 %sort.17 = (s32[256]{0:T(256)}, s32[256]{0:T(256)S(1)}) sort(s32[256]{0:T(256)S(1)} %get-tuple-element.8, s32[256]{0:T(256)S(1)} %iota.4), dimensions={0}, to_apply=%region_0.1 | sort | flops 2048 | bytes 4096 | tf_op jit(solution)/shard_map/jit(argsort)/sort | solution.py:30
  10.6 1.9 %gather_fusion = s32[256]{0:T(256)S(1)} fusion(s32[256]{0:T(256)S(1)} %get-tuple-element.7, s32[1024]{0:T(1024)S(1)} %pad_clamp_fusion), kind=kCustom, calls=%fused_computation | custom fusion | bytes 3072 | tf_op jit(solution)/shard_map/gather | solution.py:32
  12.5 0.7 all_to_all.9
  13.2 7.3 %all-to-all-start = ((s32[8,1,32]{2,1,0:T(1,128)}), s32[8,1,32]{2,1,0:T(1,128)S(1)}, u32[]{:S(2)}, u32[]{:S(2)}) async-start(s32[8,1,32]{2,1,0:T(1,128)} %all_to_all.9), calls=%async_computation | async-start | bytes 8192 | tf_op jit(solution)/shard_map/all_to_all | solution.py:35
  20.5 0.7 convert.5
  21.2 0.1 slice.23
  21.3 0.0 copy-start.1
  21.3 0.2 mul.29
  21.4 0.0 copy-done.2
  21.4 0.9 %bitcast_multiply_fusion = bf16[384,768]{1,0:T(8,128)(2,1)} fusion(bf16[48,8,6,128]{3,2,1,0:T(8,128)(2,1)S(1)} %bitcast.16, bf16[384,1280]{1,0:T(8,128)(2,1)S(1)} %copy-done.2), kind=kLoop, calls=%fused_computation.7 | loop fusion | flops 294912 | bytes 1769472 | tf_op jit(solution)/shard_map/mul | solution.py:17
  22.3 0.0 copy-done.1
  22.3 1.8 %gather_fusion.1 = bf16[256,512]{1,0:T(8,128)(2,1)} fusion(bf16[256,512]{1,0:T(8,128)(2,1)S(1)} %copy-done.1, s32[1024]{0:T(1024)S(1)} %pad_clamp_fusion), kind=kCustom, calls=%fused_computation.1 | custom fusion | bytes 525312 | tf_op jit(solution)/shard_map/gather | solution.py:31
  24.2 2.7 %all-to-all-done = s32[8,1,32]{2,1,0:T(1,128)S(1)} async-done(((s32[8,1,32]{2,1,0:T(1,128)}), s32[8,1,32]{2,1,0:T(1,128)S(1)}, u32[]{:S(2)}, u32[]{:S(2)}) %all-to-all-start) | async-done | bytes 1056 | tf_op jit(solution)/shard_map/all_to_all | solution.py:35
  26.9 3.4 %all-to-all-start.1 = ((bf16[8,32,512]{2,1,0:T(8,128)(2,1)}), bf16[8,32,512]{2,1,0:T(8,128)(2,1)S(1)}, u32[]{:S(2)}, u32[]{:S(2)}) async-start(bf16[8,32,512]{2,1,0:T(8,128)(2,1)} %bitcast.1), calls=%async_computation.1 | async-start | bytes 524288 | tf_op jit(solution)/shard_map/all_to_all | solution.py:34
  30.3 0.0 reduce-scatter.4.cloned.1.call-start
  30.3 0.1 slice_convert_fusion
  30.4 0.5 broadcast.35
  30.9 0.7 reduce.3
  31.6 0.1 reshape.52
  31.7 7.0 %all-to-all-done.1 = bf16[8,32,512]{2,1,0:T(8,128)(2,1)S(1)} async-done(((bf16[8,32,512]{2,1,0:T(8,128)(2,1)}), bf16[8,32,512]{2,1,0:T(8,128)(2,1)S(1)}, u32[]{:S(2)}, u32[]{:S(2)}) %all-to-all-start.1) | async-done | bytes 262176 | tf_op jit(solution)/shard_map/all_to_all | solution.py:34
  38.7 0.0 copy-start.3
  38.7 2.4 %scatter_custom_fusion = f32[384,512]{1,0:T(8,128)S(1)} fusion(f32[384,512]{1,0:T(8,128)S(1)} %slice_convert_fusion, s32[256]{0:T(256)S(1)} %bitcast.22, bf16[256,512]{1,0:T(8,128)(2,1)S(1)} %bitcast.19), kind=kCustom, calls=%fused_computation.8 | custom fusion | flops 262144 | bytes 1048576 | tf_op jit(solution)/shard_map/scatter-add | solution.py:40
  41.1 0.2 mul.26
  41.3 0.1 bitcast_multiply_fusion.1
  41.4 0.0 copy-done
  41.4 0.0 copy-done.3
  41.4 0.7 convolution_convert_fusion
  42.1 0.9 %copy.6 = bf16[384,512]{0,1:T(8,128)(2,1)} copy(bf16[384,512]{1,0:T(8,128)(2,1)S(1)} %convolution_convert_fusion) | data formatting | bytes 786432
  43.0 0.0 reduce-scatter.4.cloned.1.call-update
  43.0 19.8 %reduce-scatter.4.cloned.1.call-done = bf16[128,384]{1,0:T(8,128)(2,1)} async-done(((bf16[512,384]{1,0:T(8,128)(2,1)}), bf16[128,384]{1,0:T(8,128)(2,1)}) %reduce-scatter.4.cloned.1.call-update) | async-done | bytes 98320
  62.8 1.6 %copy.7 = bf16[384,128]{1,0:T(8,128)(2,1)} copy(bf16[384,128]{0,1:T(8,128)(2,1)} %bitcast.20) | data formatting | bytes 196608
  (4 shorter events, 0.0 us)
Async XLA Ops:
  6.5 34.8 %copy-start = (bf16[1280,512]{1,0:T(8,128)(2,1)S(1)}, bf16[1280,512]{1,0:T(8,128)(2,1)}, u32[]{:S(2)}) copy-start(bf16[1280,512]{1,0:T(8,128)(2,1)} %param.9) | copy-start | bytes 3932164
  6.5 14.9 %copy-start.2 = (bf16[384,1280]{1,0:T(8,128)(2,1)S(1)}, bf16[384,1280]{1,0:T(8,128)(2,1)}, u32[]{:S(2)}) copy-start(bf16[384,1280]{1,0:T(8,128)(2,1)} %param.5) | copy-start | bytes 2949124
  13.2 13.7 %all-to-all-start = ((s32[8,1,32]{2,1,0:T(1,128)}), s32[8,1,32]{2,1,0:T(1,128)S(1)}, u32[]{:S(2)}, u32[]{:S(2)}) async-start(s32[8,1,32]{2,1,0:T(1,128)} %all_to_all.9), calls=%async_computation | async-start | bytes 8192 | tf_op jit(solution)/shard_map/all_to_all | solution.py:35
  21.3 1.1 %copy-start.1 = (bf16[256,512]{1,0:T(8,128)(2,1)S(1)}, bf16[256,512]{1,0:T(8,128)(2,1)}, u32[]{:S(2)}) copy-start(bf16[256,512]{1,0:T(8,128)(2,1)} %param.6) | copy-start | bytes 786436
  26.9 11.8 %all-to-all-start.1 = ((bf16[8,32,512]{2,1,0:T(8,128)(2,1)}), bf16[8,32,512]{2,1,0:T(8,128)(2,1)S(1)}, u32[]{:S(2)}, u32[]{:S(2)}) async-start(bf16[8,32,512]{2,1,0:T(8,128)(2,1)} %bitcast.1), calls=%async_computation.1 | async-start | bytes 524288 | tf_op jit(solution)/shard_map/all_to_all | solution.py:34
  30.3 32.6 %reduce-scatter.4.cloned.1.call-start = ((), (), s32[]{:S(2)}) async-start(), calls=%async_computation.3 | async-start | bytes 491520
  38.7 2.7 %copy-start.3 = (bf16[384,768]{1,0:T(8,128)(2,1)S(1)}, bf16[384,768]{1,0:T(8,128)(2,1)}, u32[]{:S(2)}) copy-start(bf16[384,768]{1,0:T(8,128)(2,1)} %bitcast_multiply_fusion) | copy-start | bytes 1769476
Sparse Core Ops, SparseCore 0:
  43.1 19.6 reduce-scatter.3
where the time goes:
time: 71.7 us; the launch traced here: 71.3 us
  waiting for transfers between devices  29.5 us (41%)
  between operations  13.5 us (19%)
  starting transfers between devices  10.7 us (15%)
  other arithmetic  8.85 us (12%)
  local copies, waits for them, and re-layouts  8.04 us (11%)
    unnamed x2, waiting for transfers between devices  19.9 us
    all_to_all x1, starting transfers between devices, local(): lax.all_to_all(places, 'wide', split_axis=0, concat_axis=0, tiled=True)  7.28 us
    all_to_all x1, waiting for transfers between devices, local(): lax.all_to_all(outgoing, 'wide', split_axis=0, concat_axis=0, tiled=True)  6.99 us
    all_to_all x1, starting transfers between devices, local(): lax.all_to_all(outgoing, 'wide', split_axis=0, concat_axis=0, tiled=True)  3.41 us
    sort x1, other arithmetic, local(): ordering = jnp.argsort(target, stable=True)  3.17 us
    all_to_all x1, waiting for transfers between devices, local(): lax.all_to_all(places, 'wide', split_axis=0, concat_axis=0, tiled=True)  2.69 us
    unnamed x10, local copies, waits for them, and re-layouts  2.56 us
    scatter-add x1, other arithmetic, local(): added_sum = jnp.zeros((rows_dev, touched_cols), jnp.float32).at[arrived_r...  2.43 us
  transfers between devices with their start and end apart: 3, of which 3 were waited for; matrix products, arithmetic and copies ran while one was open for 7% of the time, Pallas kernels for 0%

commit v1 on v0

v1 whole, which is shorter than its diff:
```python
import functools

import jax
import jax.numpy as jnp
from jax import lax
from jax.experimental import pallas as pl
from jax.experimental.pallas import tpu as pltpu
from jax.sharding import PartitionSpec as P

TILE = 128
GROUP = 8
MESH = pl.DeviceIdType.MESH
F32 = jnp.float32
BF16 = jnp.bfloat16


def repeat(count, body):
    if count == 1:
        body(0)
    else:
        lax.fori_loop(0, count, lambda i, carry: (body(i), carry)[1], 0)


def iota(shape, dim):
    return lax.broadcasted_iota(jnp.int32, shape, dim)


def kernel(
    wide, narrow, per_peer, mask_rows,
    parent_in, child_in, map_in, mask_in, probes_in,
    out_ref,
    parent, child, cmap, mask, probes,
    mask_all, pick, sorted_rows, places_out, places_in, scaled,
    f_own, f_core, f_send, f_x,
    z_own, z_core, z_send, z_x, z_out, z_in,
    load_sem, mask_send, mask_recv, place_send, place_recv,
    z_out_send, z_in_recv, pair_send, pair_recv,
):
    rows, cols = parent.shape
    kids, touched = child.shape
    slots = GROUP * per_peer
    groups = wide // GROUP
    row_tile = rows // mask.shape[0]
    me_w = lax.axis_index("wide")
    me_n = lax.axis_index("narrow")
    core = lax.rem(me_n, 2)
    along = lax.div(me_n, 2)
    core_peer = (me_w, me_n + 1 - 2 * core)
    x_peer = (me_w, lax.rem(me_n + 2, narrow))

    def each_peer(fn):
        def one(k):
            fn(lax.rem(me_w + k, wide))

        if wide <= GROUP:
            for k in range(1, wide):
                one(k)
        else:
            lax.fori_loop(1, wide, lambda k, carry: (one(k), carry)[1], 0)

    loads = [
        pltpu.make_async_copy(src, dst, load_sem.at[i])
        for i, (src, dst) in enumerate(
            ((map_in, cmap), (mask_in, mask), (child_in, child), (probes_in, probes), (parent_in, parent))
        )
    ]
    for load in loads:
        load.start()

    barrier = pltpu.get_barrier_semaphore()
    each_peer(
        lambda w: pl.semaphore_signal(barrier, inc=1, device_id=(w, me_n), device_id_type=MESH)
    )
    for peer in (core_peer, x_peer):
        pl.semaphore_signal(barrier, inc=1, device_id=peer, device_id_type=MESH)

    def remote(src, dst, send, recv, device):
        return pltpu.make_async_remote_copy(
            src_ref=src, dst_ref=dst, send_sem=send, recv_sem=recv,
            device_id=device, device_id_type=MESH,
        )

    def block_at(index, size):
        return pl.ds(pl.multiple_of(index * size, size), size)

    loads[0].wait()
    child_rows = cmap[...]

    def order_group(g):
        first = g * GROUP
        low = (iota((2 * GROUP, 1), 0) + first) * rows
        chosen = (child_rows >= low) & (child_rows < low + rows)
        ones = jnp.where(chosen, 1.0, 0.0)
        before = []
        step = min(kids, 256)
        for start in range(0, kids, step):
            upper = iota((kids, step), 0) < iota((kids, step), 1) + start
            before.append(
                jnp.dot(
                    ones.astype(BF16),
                    jnp.where(upper, 1.0, 0.0).astype(BF16),
                    preferred_element_type=F32,
                )
            )
        rank = before[0] if len(before) == 1 else jnp.concatenate(before, axis=1)
        rank = jnp.where(chosen, rank, -1.0)
        wanted = iota((per_peer, kids), 0).astype(F32)
        base = jnp.zeros((1, kids), jnp.int32)
        for w in range(GROUP):
            here = rank[w : w + 1, :]
            pick[pl.ds(w * per_peer, per_peer), :] = jnp.where(here == wanted, 1.0, 0.0).astype(BF16)
            base = jnp.where(here >= 0.0, (first + w) * rows, base)
        local = child_rows - base
        high = (local >> 4).astype(F32)
        less = (local & 15).astype(F32)
        line = iota((TILE, kids), 0)
        coded = jnp.where(line == 0, high, jnp.where(line == 1, less, 0.0)).astype(BF16)
        places_out[block_at(g, slots), :] = lax.dot_general(
            pick[...], coded, (((1,), (1,)), ((), ())), preferred_element_type=F32
        ).astype(BF16)

    def sort_group(g):
        sorted_rows[block_at(g, slots), :] = jnp.dot(
            pick[...], child[...], preferred_element_type=F32
        ).astype(BF16)

    if groups == 1:
        order_group(0)
    else:
        loads[2].wait()

        def both(g):
            order_group(g)
            sort_group(g)

        repeat(groups, both)

    loads[1].wait()
    padded = jnp.zeros(mask_all.shape[1:], F32)
    mask_all[me_w] = padded.astype(BF16)
    mask_all[me_w, : mask.shape[0], : mask.shape[1]] = mask[...].astype(F32).astype(BF16)

    pl.semaphore_wait(barrier, wide + 1)

    def mask_copy(sender, w):
        return remote(
            mask_all.at[sender], mask_all.at[sender], mask_send.at[w], mask_recv.at[sender], (w, me_n)
        )

    def place_copy(sender, w):
        return remote(
            places_out.at[block_at(w, per_peer)],
            places_in.at[block_at(sender, per_peer)],
            place_send.at[w], place_recv.at[sender], (w, me_n),
        )

    each_peer(lambda w: mask_copy(me_w, w).start())
    each_peer(lambda w: place_copy(me_w, w).start())
    places_in[block_at(me_w, per_peer), :] = places_out[block_at(me_w, per_peer), :]

    if groups == 1:
        loads[2].wait()
        sort_group(0)

    loads[3].wait()
    loads[4].wait()
    part = 384 if rows % 384 == 0 else rows
    my_mask = mask_all[me_w]

    def parent_part(i):
        at = iota((part, mask_rows), 0) + i * part
        tile = iota((part, mask_rows), 1) * row_tile
        spread = jnp.where((at >= tile) & (at < tile + row_tile), 1.0, 0.0).astype(BF16)
        kept = jnp.dot(spread, my_mask, preferred_element_type=F32).astype(BF16)
        here = block_at(i, part)
        blocks = [
            parent[here, t * TILE : (t + 1) * TILE] * kept[:, t : t + 1]
            for t in range(cols // TILE)
        ]
        product = jnp.dot(
            jnp.concatenate(blocks, axis=1), probes[...], preferred_element_type=F32
        ).astype(BF16)
        for n in range(narrow):
            f_own[n % 2, n // 2, here, :] = product[:, n * TILE : (n + 1) * TILE]

    repeat(rows // part, parent_part)
    f_pair = remote(f_own.at[1 - core], f_core, pair_send.at[0], pair_recv.at[0], core_peer)
    f_pair.start()

    each_peer(lambda w: mask_copy(w, w).wait_recv())

    def child_group(g):
        here = block_at(g, slots)
        place = places_out[here, :].astype(F32)
        place = place[:, 0:1] * 16.0 + place[:, 1:2]
        lane = iota((slots, GROUP * mask_rows), 1)
        peer = iota((slots, GROUP * mask_rows), 0) >> (per_peer.bit_length() - 1)
        shift = mask_rows.bit_length() - 1
        tile = ((lane & (mask_rows - 1)) * row_tile).astype(F32)
        same = ((lane >> shift) == peer) & (place >= tile) & (place < tile + row_tile)
        table = mask_all[pl.ds(g * GROUP, GROUP)].reshape(GROUP * mask_rows, TILE)
        kept = jnp.dot(
            jnp.where(same, 1.0, 0.0).astype(BF16), table, preferred_element_type=F32
        ).astype(BF16)
        for t in range(touched // TILE):
            span = slice(t * TILE, (t + 1) * TILE)
            scaled[:, span] = sorted_rows[here, span] * kept[:, t : t + 1]
        product = jnp.dot(
            scaled[...], probes[:touched, :], preferred_element_type=F32
        ).astype(BF16)
        for n in range(narrow):
            z_own[n % 2, n // 2, here, :] = product[:, n * TILE : (n + 1) * TILE]

    repeat(groups, child_group)
    z_pair = remote(z_own.at[1 - core], z_core, pair_send.at[1], pair_recv.at[1], core_peer)
    z_pair.start()

    f_pair.wait_recv()
    f_send[...] = (f_own[core, 1 - along].astype(F32) + f_core[1 - along].astype(F32)).astype(BF16)
    z_pair.wait_recv()
    z_send[...] = (z_own[core, 1 - along].astype(F32) + z_core[1 - along].astype(F32)).astype(BF16)
    z_cross = remote(z_send, z_x, pair_send.at[2], pair_recv.at[2], x_peer)
    z_cross.start()
    f_cross = remote(f_send, f_x, pair_send.at[3], pair_recv.at[3], x_peer)
    f_cross.start()
    each_peer(lambda w: place_copy(w, w).wait_recv())
    z_cross.wait_recv()
    z_out[...] = (
        z_own[core, along].astype(F32) + z_core[along].astype(F32) + z_x[...].astype(F32)
    ).astype(BF16)

    def z_copy(sender, w):
        return remote(
            z_out.at[block_at(w, per_peer)],
            z_in.at[block_at(sender, per_peer)],
            z_out_send.at[w], z_in_recv.at[sender], (w, me_n),
        )

    each_peer(lambda w: z_copy(me_w, w).start())
    z_in[block_at(me_w, per_peer), :] = z_out[block_at(me_w, per_peer), :]

    f_cross.wait_recv()
    total = f_own[core, along].astype(F32) + f_core[along].astype(F32) + f_x[...].astype(F32)
    each_peer(lambda w: z_copy(w, w).wait_recv())
    for g in range(groups):
        place = places_in[g * slots : (g + 1) * slots, :].astype(F32)
        place = place[:, 0:1] * 16.0 + place[:, 1:2]
        lands = jnp.where(place == iota((slots, rows), 1).astype(F32), 1.0, 0.0).astype(BF16)
        total = total + lax.dot_general(
            lands, z_in[g * slots : (g + 1) * slots, :], (((0,), (0,)), ((), ())),
            preferred_element_type=F32,
        )
    out_ref[...] = total.astype(out_ref.dtype)

    each_peer(lambda w: mask_copy(me_w, w).wait_send())
    each_peer(lambda w: place_copy(me_w, w).wait_send())
    each_peer(lambda w: z_copy(me_w, w).wait_send())
    for copy in (f_pair, z_pair, z_cross, f_cross):
        copy.wait_send()


def local(wide, narrow, parent_front, child_updates, child_map, tile_mask, probes):
    rows, cols = parent_front.shape
    kids, touched = child_updates.shape
    per_peer = kids // wide
    probe_cols = probes.shape[1]
    mask_rows = 16 * pl.cdiv(tile_mask.shape[0], 16)
    vmem = pltpu.VMEM
    dma = pltpu.SemaphoreType.DMA
    return pl.pallas_call(
        functools.partial(kernel, wide, narrow, per_peer, mask_rows),
        out_shape=jax.ShapeDtypeStruct((rows, probe_cols // narrow), BF16),
        in_specs=[pl.BlockSpec(memory_space=pl.ANY)] * 5,
        out_specs=pl.BlockSpec(memory_space=pltpu.VMEM),
        scratch_shapes=[
            vmem((rows, cols), BF16),
            vmem((kids, touched), BF16),
            vmem((1, kids), jnp.int32),
            vmem(tile_mask.shape, jnp.int32),
            vmem(probes.shape, BF16),
            vmem((wide, mask_rows, TILE), BF16),
            vmem((GROUP * per_peer, kids), BF16),
            vmem((kids, touched), BF16),
            vmem((kids, TILE), BF16),
            vmem((kids, TILE), BF16),
            vmem((GROUP * per_peer, touched), BF16),
            vmem((2, 2, rows, TILE), BF16),
            vmem((2, rows, TILE), BF16),
            vmem((rows, TILE), BF16),
            vmem((rows, TILE), BF16),
            vmem((2, 2, kids, TILE), BF16),
            vmem((2, kids, TILE), BF16),
            vmem((kids, TILE), BF16),
            vmem((kids, TILE), BF16),
            vmem((kids, TILE), BF16),
            vmem((kids, TILE), BF16),
            dma((5,)),
            dma((wide,)),
            dma((wide,)),
            dma((wide,)),
            dma((wide,)),
            dma((wide,)),
            dma((wide,)),
            dma((4,)),
            dma((4,)),
        ],
        compiler_params=pltpu.CompilerParams(
            collective_id=0, has_side_effects=True, vmem_limit_bytes=56 * 1024 * 1024
        ),
    )(parent_front, child_updates, child_map.reshape(1, -1), tile_mask, probes)


def solution(mesh):
    placed = (
        P("wide", "narrow"),
        P("wide", "narrow"),
        P("wide"),
        P("wide", "narrow"),
        P("narrow", None),
    )
    return jax.shard_map(
        functools.partial(local, mesh.shape["wide"], mesh.shape["narrow"]),
        mesh=mesh, in_specs=placed, out_specs=P("wide", "narrow"), check_vma=False,
    )
```

time: 71.7 us -> 22.1 us (0.31)
  waiting for transfers between devices: 29.5 us -> 0 us
  Pallas kernels: 0 us -> 20.4 us
  between operations: 13.5 us -> 0.01 us
  starting transfers between devices: 10.7 us -> 0 us
  other arithmetic: 8.85 us -> 0 us
  local copies, waits for them, and re-layouts: 8.04 us -> 1.54 us
    pallas_call x0 -> x1, Pallas kernels: none -> 20.4 us  [local(): pl.pallas_call(functools.partial(kernel, wide, narrow, per_peer, mask_row...]
    unnamed x2 -> x0, waiting for transfers between devices: 19.9 us -> none
    all_to_all x2 -> x0, starting transfers between devices: 10.7 us -> none  [the longest x1 7.28 us: local(): lax.all_to_all(places, 'wide', split_axis=0, concat_axis=0, tiled=True)]
    all_to_all x2 -> x0, waiting for transfers between devices: 9.68 us -> none  [the longest x1 6.99 us: local(): lax.all_to_all(outgoing, 'wide', split_axis=0, concat_axis=0, tiled=True)]
    gather x2 -> x0, local copies, waits for them, and re-layouts: 3.78 us -> none  [the longest x1 1.94 us: local(): (child_map - target * rows_dev)[ordering].reshape(wide_count, per_peer)]
    sort x1 -> x0, other arithmetic: 3.17 us -> none  [local(): ordering = jnp.argsort(target, stable=True)]
    scatter-add x1 -> x0, other arithmetic: 2.43 us -> none  [local(): added_sum = jnp.zeros((rows_dev, touched_cols), jnp.float32).at[arrived_r...]
    all_to_all x2 -> x0, local copies, waits for them, and re-layouts: 1.19 us -> none  [local(): lax.all_to_all(places, 'wide', split_axis=0, concat_axis=0, tiled=True)]
  transfers between devices with their start and end apart: 3 -> 0, of which waited for: 3 -> 0; matrix products, arithmetic and copies ran while one was open for 7% -> 0% of each run, Pallas kernels for 0% -> 0%
where the time goes in v1:
time: 22.1 us; the launch traced here: 22 us
  Pallas kernels  20.4 us (92%)
  local copies, waits for them, and re-layouts  1.54 us (7%)
    pallas_call x1, Pallas kernels, local(): pl.pallas_call(functools.partial(kernel, wide, narrow, per_peer, mask_row...  20.4 us
    unnamed x1, local copies, waits for them, and re-layouts  1.54 us

profile of v1, /device:TPU:0, one launch (start us, length us, event | category | flops | bytes accessed | tf_op | source)
XLA Modules:
  0.0 22.0 jit_solution(3854132034766103473)
XLA Ops:
  0.0 20.4 %shard_map.55 = bf16[384,128]{1,0:T(8,128)(2,1)} custom-call(bf16[384,1280]{1,0:T(8,128)(2,1)} %parent_in.1, bf16[256,512]{1,0:T(8,128)(2,1)} %child_in.1, s32[1,256]{1,0:T(1,128)} %bitcast.1, s32[12,10]{1,0:T(8,128)} %mask_in.1, bf16[1280,512]{1,0:T(8,128)(2,1)} %probes_in.1), custom_call_target="tpu_custom_call" | custom-call | tf_op jit(solution)/shard_map/pallas_call | solution.py:270
  20.4 1.5 %copy.7 = bf16[384,128]{1,0:T(8,128)(2,1)} copy(bf16[384,128]{1,0:T(8,128)(2,1)} %shard_map.55) | data formatting | bytes 196608

commit v2 on v1

v2 whole, which is shorter than its diff:
```python
import functools

import jax
import jax.numpy as jnp
from jax import lax
from jax.experimental import pallas as pl
from jax.experimental.pallas import tpu as pltpu
from jax.sharding import PartitionSpec as P

TILE = 128
GROUP = 8
MESH = pl.DeviceIdType.MESH
F32 = jnp.float32
BF16 = jnp.bfloat16


def repeat(count, body):
    if count == 1:
        body(0)
    else:
        lax.fori_loop(0, count, lambda i, carry: (body(i), carry)[1], 0)


def iota(shape, dim):
    return lax.broadcasted_iota(jnp.int32, shape, dim)


def kernel(
    wide, narrow, per_peer, mask_rows,
    parent_in, child_in, map_in, mask_in, probes_in,
    out_ref,
    parent, child, cmap, mask, probes, mask_pad,
    msg_out, msg_in, pick, sorted_rows, lands,
    f_own, f_core, f_send, f_x,
    z_own, z_core, z_out, z_in,
    load_sem, msg_sem, z_sem, pair_send, pair_recv,
):
    rows, cols = parent.shape
    kids, touched = child.shape
    slots = GROUP * per_peer
    groups = wide // GROUP
    row_tile = rows // mask.shape[0]
    me_w = lax.axis_index("wide")
    me_n = lax.axis_index("narrow")
    core = lax.rem(me_n, 2)
    along = lax.div(me_n, 2)
    core_peer = (me_w, me_n + 1 - 2 * core)
    x_narrow = lax.rem(me_n + 2, narrow)
    x_peer = (me_w, x_narrow)

    def each_peer(fn, first=1):
        def one(k):
            fn(lax.rem(me_w + k, wide))

        if wide <= GROUP:
            for k in range(first, wide):
                one(k)
        else:
            lax.fori_loop(first, wide, lambda k, carry: (one(k), carry)[1], 0)

    def block_at(index, size):
        return pl.ds(pl.multiple_of(index * size, size), size)

    pairs = [(map_in, cmap), (mask_in, mask), (child_in, child), (parent_in, parent)]
    for n in range(narrow):
        pairs.append(
            (
                probes_in.at[:, n * TILE : (n + 1) * TILE],
                probes.at[n % 2, :, n // 2 * TILE : (n // 2 + 1) * TILE],
            )
        )
    loads = [
        pltpu.make_async_copy(src, dst, load_sem.at[i]) for i, (src, dst) in enumerate(pairs)
    ]
    for load in loads:
        load.start()

    barrier = pltpu.get_barrier_semaphore()

    def greet(device):
        pl.semaphore_signal(barrier, inc=1, device_id=device, device_id_type=MESH)

    greet(core_peer)
    each_peer(lambda w: greet((w, me_n)))
    each_peer(lambda w: greet((w, x_narrow)), first=0)

    def remote(src, dst, send, recv, device):
        return pltpu.make_async_remote_copy(
            src_ref=src, dst_ref=dst, send_sem=send, recv_sem=recv,
            device_id=device, device_id_type=MESH,
        )

    loads[0].wait()
    child_rows = cmap[...]

    def order_group(g):
        first = g * GROUP
        low = (iota((2 * GROUP, 1), 0) + first) * rows
        chosen = (child_rows >= low) & (child_rows < low + rows)
        ones = jnp.where(chosen, 1.0, 0.0)
        before = []
        step = min(kids, 256)
        for start in range(0, kids, step):
            upper = iota((kids, step), 0) < iota((kids, step), 1) + start
            before.append(
                jnp.dot(
                    ones.astype(BF16),
                    jnp.where(upper, 1.0, 0.0).astype(BF16),
                    preferred_element_type=F32,
                )
            )
        rank = before[0] if len(before) == 1 else jnp.concatenate(before, axis=1)
        rank = jnp.where(chosen, rank, -1.0)
        wanted = iota((per_peer, kids), 0).astype(F32)
        base = jnp.zeros((1, kids), jnp.int32)
        for w in range(GROUP):
            here = rank[w : w + 1, :]
            pick[pl.ds(w * per_peer, per_peer), :] = jnp.where(here == wanted, 1.0, 0.0).astype(BF16)
            base = jnp.where(here >= 0.0, (first + w) * rows, base)
        local = child_rows - base
        high = (local >> 4).astype(F32)
        less = (local & 15).astype(F32)
        line = iota((TILE, kids), 0)
        coded = jnp.where(line == 0, high, jnp.where(line == 1, less, 0.0)).astype(BF16)
        places = lax.dot_general(
            pick[...], coded, (((1,), (1,)), ((), ())), preferred_element_type=F32
        ).astype(BF16)
        msg_out[pl.ds(first, GROUP), :per_peer, :] = places.reshape(GROUP, per_peer, TILE)

    def sort_group(g):
        sorted_rows[block_at(g, slots), :] = jnp.dot(
            pick[...], child[...], preferred_element_type=F32
        ).astype(BF16)

    if groups == 1:
        order_group(0)
    else:
        loads[2].wait()

        def both(g):
            order_group(g)
            sort_group(g)

        repeat(groups, both)

    loads[1].wait()
    mask_pad[...] = jnp.zeros(mask_pad.shape, BF16)
    mask_pad[: mask.shape[0], : mask.shape[1]] = mask[...].astype(F32).astype(BF16)
    my_mask = mask_pad[...]
    repeat(groups, lambda g: msg_out.__setitem__(
        (pl.ds(g * GROUP, GROUP), slice(per_peer, per_peer + mask_rows)),
        jnp.broadcast_to(my_mask[None], (GROUP, mask_rows, TILE)),
    ))

    pl.semaphore_wait(barrier, 2 * wide)

    each_peer(
        lambda w: remote(
            msg_out.at[w], msg_in.at[me_w], msg_sem.at[0], msg_sem.at[1], (w, me_n)
        ).start()
    )
    msg_in[me_w] = msg_out[me_w]
    messages = remote(
        msg_out.at[pl.ds(0, wide - 1)], msg_in.at[pl.ds(0, wide - 1)],
        msg_sem.at[0], msg_sem.at[1], x_peer,
    )

    if groups == 1:
        loads[2].wait()
        sort_group(0)

    part = 384 if rows % 384 == 0 else rows

    def parent_mask(i):
        at = iota((part, mask_rows), 0) + i * part
        tile = iota((part, mask_rows), 1) * row_tile
        spread = jnp.where((at >= tile) & (at < tile + row_tile), 1.0, 0.0).astype(BF16)
        kept = jnp.dot(spread, my_mask, preferred_element_type=F32).astype(BF16)
        here = block_at(i, part)
        for t in range(cols // TILE):
            span = slice(t * TILE, (t + 1) * TILE)
            parent[here, span] = parent[here, span] * kept[:, t : t + 1]

    def parent_half(half):
        def one(i):
            product = jnp.dot(
                parent[block_at(i, part), :], probes[half], preferred_element_type=F32
            ).astype(BF16)
            for x in range(2):
                f_own[half, x, block_at(i, part), :] = product[:, x * TILE : (x + 1) * TILE]

        repeat(rows // part, one)

    loads[3].wait()
    repeat(rows // part, parent_mask)
    for load in loads[4:]:
        load.wait()
    parent_half(1 - core)
    f_pair = remote(f_own.at[1 - core], f_core, pair_send.at[0], pair_recv.at[0], core_peer)
    f_pair.start()
    parent_half(core)

    shift = mask_rows.bit_length() - 1

    def landing(g):
        place = msg_out[pl.ds(g * GROUP, GROUP), :per_peer, :].reshape(slots, TILE).astype(F32)
        place = place[:, 0:1] * 16.0 + place[:, 1:2]
        lane = iota((slots, GROUP * mask_rows), 1)
        peer = iota((slots, GROUP * mask_rows), 0) >> (per_peer.bit_length() - 1)
        tile = ((lane & (mask_rows - 1)) * row_tile).astype(F32)
        same = ((lane >> shift) == peer) & (place >= tile) & (place < tile + row_tile)
        return jnp.where(same, 1.0, 0.0).astype(BF16)

    def child_mask(g, tiles):
        table = msg_in[pl.ds(g * GROUP, GROUP), per_peer:, :].reshape(GROUP * mask_rows, TILE)
        kept = jnp.dot(tiles, table, preferred_element_type=F32).astype(BF16)
        here = block_at(g, slots)
        for t in range(touched // TILE):
            span = slice(t * TILE, (t + 1) * TILE)
            sorted_rows[here, span] = sorted_rows[here, span] * kept[:, t : t + 1]

    def child_half(half):
        def one(g):
            product = jnp.dot(
                sorted_rows[block_at(g, slots), :], probes[half, :touched, :],
                preferred_element_type=F32,
            ).astype(BF16)
            for x in range(2):
                z_own[half, x, block_at(g, slots), :] = product[:, x * TILE : (x + 1) * TILE]

        repeat(groups, one)

    if groups == 1:
        tiles = landing(0)
        messages.wait_recv()
        child_mask(0, tiles)
    else:
        messages.wait_recv()
        repeat(groups, lambda g: child_mask(g, landing(g)))
    child_half(1 - core)
    z_pair = remote(z_own.at[1 - core], z_core, pair_send.at[1], pair_recv.at[1], core_peer)
    z_pair.start()
    child_half(core)

    f_pair.wait_recv()
    f_send[...] = (f_own[core, 1 - along].astype(F32) + f_core[1 - along].astype(F32)).astype(BF16)
    f_cross = remote(f_send, f_x, pair_send.at[2], pair_recv.at[2], x_peer)
    f_cross.start()
    z_pair.wait_recv()

    def z_sum(x):
        z_out[block_at(x, kids), :] = (
            z_own[core, x].astype(F32) + z_core[x].astype(F32)
        ).astype(BF16)

    def z_start(x, n, w):
        remote(
            z_out.at[block_at(x * wide + w, per_peer)],
            z_in.at[block_at(along * wide + me_w, per_peer)],
            z_sem.at[0], z_sem.at[1], (w, n),
        ).start()

    z_sum(1 - along)
    each_peer(lambda w: z_start(1 - along, x_narrow, w), first=0)
    z_sum(along)
    each_peer(lambda w: z_start(along, me_n, w))
    mine = block_at(along * wide + me_w, per_peer)
    z_in[mine, :] = z_out[mine, :]
    most = pl.ds(0, (2 * wide - 1) * per_peer)
    arrivals = remote(z_out.at[most], z_in.at[most], z_sem.at[0], z_sem.at[1], x_peer)

    for g in range(groups):
        place = msg_in[g * GROUP : (g + 1) * GROUP, :per_peer, :].reshape(slots, TILE)
        lane = iota((2 * GROUP, TILE), 1)
        weigh = jnp.where(lane == 0, 16.0, jnp.where(lane == 1, 1.0, 0.0)).astype(BF16)
        place = lax.dot_general(
            weigh, place, (((1,), (1,)), ((), ())), preferred_element_type=F32
        )[0:1, :]
        lands[:, g * slots : (g + 1) * slots] = jnp.where(
            place == iota((rows, slots), 0).astype(F32), 1.0, 0.0
        ).astype(BF16)
    f_cross.wait_recv()
    total = f_own[core, along].astype(F32) + f_core[along].astype(F32) + f_x[...].astype(F32)
    arrivals.wait_recv()
    both_chips = jnp.concatenate([z_in[:kids, :], z_in[kids:, :]], axis=1)
    added = jnp.dot(lands[...], both_chips, preferred_element_type=F32)
    out_ref[...] = (total + (added[:, :TILE] + added[:, TILE:])).astype(out_ref.dtype)

    messages.wait_send()
    arrivals.wait_send()
    for copy in (f_pair, z_pair, f_cross):
        copy.wait_send()


def local(wide, narrow, parent_front, child_updates, child_map, tile_mask, probes):
    rows, cols = parent_front.shape
    kids, touched = child_updates.shape
    per_peer = kids // wide
    probe_cols = probes.shape[1]
    mask_rows = 16 * pl.cdiv(tile_mask.shape[0], 16)
    shapes = [
        ((rows, cols), BF16),
        ((kids, touched), BF16),
        ((1, kids), jnp.int32),
        (tile_mask.shape, jnp.int32),
        ((2, cols, 2 * TILE), BF16),
        ((mask_rows, TILE), BF16),
        ((wide, per_peer + mask_rows, TILE), BF16),
        ((wide, per_peer + mask_rows, TILE), BF16),
        ((GROUP * per_peer, kids), BF16),
        ((kids, touched), BF16),
        ((rows, kids), BF16),
        ((2, 2, rows, TILE), BF16),
        ((2, rows, TILE), BF16),
        ((rows, TILE), BF16),
        ((rows, TILE), BF16),
        ((2, 2, kids, TILE), BF16),
        ((2, kids, TILE), BF16),
        ((2 * kids, TILE), BF16),
        ((2 * kids, TILE), BF16),
    ]
    dma = pltpu.SemaphoreType.DMA
    return pl.pallas_call(
        functools.partial(kernel, wide, narrow, per_peer, mask_rows),
        out_shape=jax.ShapeDtypeStruct((rows, probe_cols // narrow), BF16),
        in_specs=[pl.BlockSpec(memory_space=pltpu.HBM)] * 5,
        out_specs=pl.BlockSpec(memory_space=pltpu.VMEM),
        scratch_shapes=[pltpu.VMEM(shape, dtype) for shape, dtype in shapes]
        + [dma((8,)), dma((2,)), dma((2,)), dma((3,)), dma((3,))],
        compiler_params=pltpu.CompilerParams(
            collective_id=0, has_side_effects=True,
            vmem_limit_bytes=56 * 1024 * 1024,
        ),
    )(parent_front, child_updates, child_map.reshape(1, -1), tile_mask, probes)


def solution(mesh):
    placed = (
        P("wide", "narrow"),
        P("wide", "narrow"),
        P("wide"),
        P("wide", "narrow"),
        P("narrow", None),
    )
    return jax.shard_map(
        functools.partial(local, mesh.shape["wide"], mesh.shape["narrow"]),
        mesh=mesh, in_specs=placed, out_specs=P("wide", "narrow"), check_vma=False,
    )
```

time: 22.1 us -> 20.1 us (0.910)
  Pallas kernels: 20.4 us -> 18.3 us
    pallas_call x1, Pallas kernels: 20.4 us -> 18.3 us  [local(): pl.pallas_call(functools.partial(kernel, wide, narrow, per_peer, mask_row...]
where the time goes in v2:
time: 20.1 us; the launch traced here: 19.9 us
  Pallas kernels  18.3 us (91%)
  local copies, waits for them, and re-layouts  1.54 us (8%)
    pallas_call x1, Pallas kernels, local(): pl.pallas_call(functools.partial(kernel, wide, narrow, per_peer, mask_row...  18.3 us
    unnamed x1, local copies, waits for them, and re-layouts  1.54 us

profile of v2, /device:TPU:0, one launch (start us, length us, event | category | flops | bytes accessed | tf_op | source)
XLA Modules:
  0.0 19.9 jit_solution(1223158361255619598)
XLA Ops:
  0.0 18.3 %shard_map.55 = bf16[384,128]{1,0:T(8,128)(2,1)} custom-call(bf16[384,1280]{1,0:T(8,128)(2,1)} %parent_in.1, bf16[256,512]{1,0:T(8,128)(2,1)} %child_in.1, s32[1,256]{1,0:T(1,128)} %bitcast.1, s32[12,10]{1,0:T(8,128)} %mask_in.1, bf16[1280,512]{1,0:T(8,128)(2,1)} %probes_in.1), custom_call_target="tpu_custom_call" | custom-call | tf_op jit(solution)/shard_map/pallas_call | solution.py:323
  18.4 1.5 %copy.7 = bf16[384,128]{1,0:T(8,128)(2,1)} copy(bf16[384,128]{1,0:T(8,128)(2,1)} %shard_map.55) | data formatting | bytes 196608

commit v3 on v2

--- a/solution.py
+++ b/solution.py
@@ -33,7 +33,7 @@
     msg_out, msg_in, pick, sorted_rows, lands,
     f_own, f_core, f_send, f_x,
     z_own, z_core, z_out, z_in,
-    load_sem, msg_sem, z_sem, pair_send, pair_recv,
+    load_sem, msg_sem, z_sem, pair_send, pair_recv, ready,
 ):
     rows, cols = parent.shape
     kids, touched = child.shape
@@ -61,6 +61,15 @@
     def block_at(index, size):
         return pl.ds(pl.multiple_of(index * size, size), size)
 
+    barrier = pltpu.get_barrier_semaphore()
+
+    def greet(device):
+        pl.semaphore_signal(barrier, inc=1, device_id=device, device_id_type=MESH)
+
+    each_peer(lambda w: greet((w, me_n)))
+    greet(core_peer)
+    greet(x_peer)
+
     pairs = [(map_in, cmap), (mask_in, mask), (child_in, child), (parent_in, parent)]
     for n in range(narrow):
         pairs.append(
@@ -74,15 +83,6 @@
     ]
     for load in loads:
         load.start()
-
-    barrier = pltpu.get_barrier_semaphore()
-
-    def greet(device):
-        pl.semaphore_signal(barrier, inc=1, device_id=device, device_id_type=MESH)
-
-    greet(core_peer)
-    each_peer(lambda w: greet((w, me_n)))
-    each_peer(lambda w: greet((w, x_narrow)), first=0)
 
     def remote(src, dst, send, recv, device):
         return pltpu.make_async_remote_copy(
@@ -152,7 +152,7 @@
         jnp.broadcast_to(my_mask[None], (GROUP, mask_rows, TILE)),
     ))
 
-    pl.semaphore_wait(barrier, 2 * wide)
+    pl.semaphore_wait(barrier, wide + 1)
 
     each_peer(
         lambda w: remote(
@@ -198,7 +198,6 @@
     parent_half(1 - core)
     f_pair = remote(f_own.at[1 - core], f_core, pair_send.at[0], pair_recv.at[0], core_peer)
     f_pair.start()
-    parent_half(core)
 
     shift = mask_rows.bit_length() - 1
 
@@ -230,17 +229,22 @@
 
         repeat(groups, one)
 
+    def all_in():
+        messages.wait_recv()
+        pl.semaphore_signal(ready, inc=1, device_id=x_peer, device_id_type=MESH)
+
     if groups == 1:
         tiles = landing(0)
-        messages.wait_recv()
+        all_in()
         child_mask(0, tiles)
     else:
-        messages.wait_recv()
+        all_in()
         repeat(groups, lambda g: child_mask(g, landing(g)))
     child_half(1 - core)
     z_pair = remote(z_own.at[1 - core], z_core, pair_send.at[1], pair_recv.at[1], core_peer)
     z_pair.start()
     child_half(core)
+    parent_half(core)
 
     f_pair.wait_recv()
     f_send[...] = (f_own[core, 1 - along].astype(F32) + f_core[1 - along].astype(F32)).astype(BF16)
@@ -261,6 +265,7 @@
         ).start()
 
     z_sum(1 - along)
+    pl.semaphore_wait(ready, 1)
     each_peer(lambda w: z_start(1 - along, x_narrow, w), first=0)
     z_sum(along)
     each_peer(lambda w: z_start(along, me_n, w))
@@ -322,11 +327,11 @@
     dma = pltpu.SemaphoreType.DMA
     return pl.pallas_call(
         functools.partial(kernel, wide, narrow, per_peer, mask_rows),
-        out_shape=jax.ShapeDtypeStruct((rows, probe_cols // narrow), BF16),
+        out_shape=pltpu.VMEM((rows, probe_cols // narrow), BF16),
         in_specs=[pl.BlockSpec(memory_space=pltpu.HBM)] * 5,
         out_specs=pl.BlockSpec(memory_space=pltpu.VMEM),
         scratch_shapes=[pltpu.VMEM(shape, dtype) for shape, dtype in shapes]
-        + [dma((8,)), dma((2,)), dma((2,)), dma((3,)), dma((3,))],
+        + [dma((8,)), dma((2,)), dma((2,)), dma((3,)), dma((3,)), pltpu.SemaphoreType.REGULAR],
         compiler_params=pltpu.CompilerParams(
             collective_id=0, has_side_effects=True,
             vmem_limit_bytes=56 * 1024 * 1024,

time: 20.1 us -> 18.5 us (0.920)
  local copies, waits for them, and re-layouts: 1.54 us -> 0.64 us
  Pallas kernels: 18.3 us -> 17.7 us
    unnamed x1, local copies, waits for them, and re-layouts: 1.54 us -> 0.64 us
    pallas_call x1, Pallas kernels: 18.3 us -> 17.7 us  [local(): pl.pallas_call(functools.partial(kernel, wide, narrow, per_peer, mask_row...]
where the time goes in v3:
time: 18.5 us; the launch traced here: 18.4 us
  Pallas kernels  17.7 us (96%)
  local copies, waits for them, and re-layouts  0.64 us (3%)
    pallas_call x1, Pallas kernels, local(): pl.pallas_call(functools.partial(kernel, wide, narrow, per_peer, mask_row...  17.7 us
    unnamed x1, local copies, waits for them, and re-layouts  0.64 us

profile of v3, /device:TPU:0, one launch (start us, length us, event | category | flops | bytes accessed | tf_op | source)
XLA Modules:
  0.0 18.4 jit_solution(2010629649229819628)
XLA Ops:
  0.0 17.7 %shard_map.55 = bf16[384,128]{1,0:T(8,128)(2,1)S(1)} custom-call(bf16[384,1280]{1,0:T(8,128)(2,1)} %parent_in.1, bf16[256,512]{1,0:T(8,128)(2,1)} %child_in.1, s32[1,256]{1,0:T(1,128)} %bitcast.1, s32[12,10]{1,0:T(8,128)} %mask_in.1, bf16[1280,512]{1,0:T(8,128)(2,1)} %probes_in.1), custom_call_target="tpu_custom_call" | custom-call | tf_op jit(solution)/shard_map/pallas_call | solution.py:328
  17.7 0.6 %copy.7 = bf16[384,128]{1,0:T(8,128)(2,1)} copy(bf16[384,128]{1,0:T(8,128)(2,1)S(1)} %shard_map.55) | data formatting | bytes 196608

commit v4 on v3

--- a/solution.py
+++ b/solution.py
@@ -30,13 +30,13 @@
     parent_in, child_in, map_in, mask_in, probes_in,
     out_ref,
     parent, child, cmap, mask, probes, mask_pad,
-    msg_out, msg_in, pick, sorted_rows, lands,
+    probes_far, msg_out, msg_in, mask_far, pick, sorted_rows, lands,
     f_own, f_core, f_send, f_x,
-    z_own, z_core, z_out, z_in,
-    load_sem, msg_sem, z_sem, pair_send, pair_recv, ready,
+    z_out, z_in,
+    load_sem, msg_sem, far_sem, z_sem, pair_send, pair_recv, ready,
 ):
     rows, cols = parent.shape
-    kids, touched = child.shape
+    _, kids, touched = child.shape
     slots = GROUP * per_peer
     groups = wide // GROUP
     row_tile = rows // mask.shape[0]
@@ -44,7 +44,8 @@
     me_n = lax.axis_index("narrow")
     core = lax.rem(me_n, 2)
     along = lax.div(me_n, 2)
-    core_peer = (me_w, me_n + 1 - 2 * core)
+    core_narrow = me_n + 1 - 2 * core
+    core_peer = (me_w, core_narrow)
     x_narrow = lax.rem(me_n + 2, narrow)
     x_peer = (me_w, x_narrow)
 
@@ -67,10 +68,10 @@
         pl.semaphore_signal(barrier, inc=1, device_id=device, device_id_type=MESH)
 
     each_peer(lambda w: greet((w, me_n)))
-    greet(core_peer)
+    each_peer(lambda w: greet((w, core_narrow)), first=0)
     greet(x_peer)
 
-    pairs = [(map_in, cmap), (mask_in, mask), (child_in, child), (parent_in, parent)]
+    pairs = [(map_in, cmap), (mask_in, mask), (child_in, child.at[0]), (parent_in, parent)]
     for n in range(narrow):
         pairs.append(
             (
@@ -115,7 +116,7 @@
         base = jnp.zeros((1, kids), jnp.int32)
         for w in range(GROUP):
             here = rank[w : w + 1, :]
-            pick[pl.ds(w * per_peer, per_peer), :] = jnp.where(here == wanted, 1.0, 0.0).astype(BF16)
+            pick[block_at(first + w, per_peer), :] = jnp.where(here == wanted, 1.0, 0.0).astype(BF16)
             base = jnp.where(here >= 0.0, (first + w) * rows, base)
         local = child_rows - base
         high = (local >> 4).astype(F32)
@@ -123,25 +124,16 @@
         line = iota((TILE, kids), 0)
         coded = jnp.where(line == 0, high, jnp.where(line == 1, less, 0.0)).astype(BF16)
         places = lax.dot_general(
-            pick[...], coded, (((1,), (1,)), ((), ())), preferred_element_type=F32
+            pick[block_at(g, slots), :], coded, (((1,), (1,)), ((), ())), preferred_element_type=F32
         ).astype(BF16)
         msg_out[pl.ds(first, GROUP), :per_peer, :] = places.reshape(GROUP, per_peer, TILE)
 
-    def sort_group(g):
-        sorted_rows[block_at(g, slots), :] = jnp.dot(
-            pick[...], child[...], preferred_element_type=F32
+    def sort_group(g, source):
+        sorted_rows[block_at(g, slots), source * touched : (source + 1) * touched] = jnp.dot(
+            pick[block_at(g, slots), :], child[source], preferred_element_type=F32
         ).astype(BF16)
 
-    if groups == 1:
-        order_group(0)
-    else:
-        loads[2].wait()
-
-        def both(g):
-            order_group(g)
-            sort_group(g)
-
-        repeat(groups, both)
+    repeat(groups, order_group)
 
     loads[1].wait()
     mask_pad[...] = jnp.zeros(mask_pad.shape, BF16)
@@ -152,22 +144,40 @@
         jnp.broadcast_to(my_mask[None], (GROUP, mask_rows, TILE)),
     ))
 
-    pl.semaphore_wait(barrier, wide + 1)
+    pl.semaphore_wait(barrier, 2 * wide)
+
+    far_copies = [remote(child_in, child.at[1], far_sem.at[0], far_sem.at[1], core_peer)]
+    for x in range(2):
+        span = pl.ds(pl.multiple_of((2 * x + 1 - core) * TILE, TILE), TILE)
+        far_copies.append(
+            remote(
+                probes_in.at[:touched, span], probes_far.at[:, x * TILE : (x + 1) * TILE],
+                far_sem.at[2 + 2 * x], far_sem.at[3 + 2 * x], core_peer,
+            )
+        )
 
     each_peer(
         lambda w: remote(
             msg_out.at[w], msg_in.at[me_w], msg_sem.at[0], msg_sem.at[1], (w, me_n)
         ).start()
     )
+    for copy in far_copies:
+        copy.start()
+    each_peer(
+        lambda w: remote(
+            mask_pad, mask_far.at[me_w], msg_sem.at[2], msg_sem.at[3], (w, core_narrow)
+        ).start(),
+        first=0,
+    )
     msg_in[me_w] = msg_out[me_w]
+    masks = remote(mask_far, mask_far, msg_sem.at[2], msg_sem.at[3], core_peer)
     messages = remote(
         msg_out.at[pl.ds(0, wide - 1)], msg_in.at[pl.ds(0, wide - 1)],
         msg_sem.at[0], msg_sem.at[1], x_peer,
     )
 
-    if groups == 1:
-        loads[2].wait()
-        sort_group(0)
+    loads[2].wait()
+    repeat(groups, lambda g: sort_group(g, 0))
 
     part = 384 if rows % 384 == 0 else rows
 
@@ -198,6 +208,9 @@
     parent_half(1 - core)
     f_pair = remote(f_own.at[1 - core], f_core, pair_send.at[0], pair_recv.at[0], core_peer)
     f_pair.start()
+    parent_half(core)
+    far_copies[0].wait_recv()
+    repeat(groups, lambda g: sort_group(g, 1))
 
     shift = mask_rows.bit_length() - 1
 
@@ -212,26 +225,33 @@
 
     def child_mask(g, tiles):
         table = msg_in[pl.ds(g * GROUP, GROUP), per_peer:, :].reshape(GROUP * mask_rows, TILE)
-        kept = jnp.dot(tiles, table, preferred_element_type=F32).astype(BF16)
+        far = mask_far[pl.ds(g * GROUP, GROUP)].reshape(GROUP * mask_rows, TILE)
         here = block_at(g, slots)
-        for t in range(touched // TILE):
-            span = slice(t * TILE, (t + 1) * TILE)
-            sorted_rows[here, span] = sorted_rows[here, span] * kept[:, t : t + 1]
-
-    def child_half(half):
-        def one(g):
-            product = jnp.dot(
-                sorted_rows[block_at(g, slots), :], probes[half, :touched, :],
-                preferred_element_type=F32,
-            ).astype(BF16)
-            for x in range(2):
-                z_own[half, x, block_at(g, slots), :] = product[:, x * TILE : (x + 1) * TILE]
-
-        repeat(groups, one)
+        count = touched // TILE
+        for source, part_table in enumerate((table, far)):
+            kept = jnp.dot(tiles, part_table, preferred_element_type=F32).astype(BF16)
+            for t in range(count):
+                span = slice((source * count + t) * TILE, (source * count + t + 1) * TILE)
+                sorted_rows[here, span] = sorted_rows[here, span] * kept[:, t : t + 1]
+
+    def child_product(g):
+        here = block_at(g, slots)
+        product = jnp.dot(
+            sorted_rows[here, :touched], probes[core, :touched, :], preferred_element_type=F32
+        ) + jnp.dot(sorted_rows[here, touched:], probes_far[...], preferred_element_type=F32)
+        product = product.astype(BF16)
+        for x in range(2):
+            z_out[block_at(x * groups + g, slots), :] = product[:, x * TILE : (x + 1) * TILE]
+
+    f_pair.wait_recv()
+    f_send[...] = (f_own[core, 1 - along].astype(F32) + f_core[1 - along].astype(F32)).astype(BF16)
+    f_cross = remote(f_send, f_x, pair_send.at[1], pair_recv.at[1], x_peer)
+    f_cross.start()
 
     def all_in():
         messages.wait_recv()
         pl.semaphore_signal(ready, inc=1, device_id=x_peer, device_id_type=MESH)
+        masks.wait_recv()
 
     if groups == 1:
         tiles = landing(0)
@@ -240,22 +260,9 @@
     else:
         all_in()
         repeat(groups, lambda g: child_mask(g, landing(g)))
-    child_half(1 - core)
-    z_pair = remote(z_own.at[1 - core], z_core, pair_send.at[1], pair_recv.at[1], core_peer)
-    z_pair.start()
-    child_half(core)
-    parent_half(core)
-
-    f_pair.wait_recv()
-    f_send[...] = (f_own[core, 1 - along].astype(F32) + f_core[1 - along].astype(F32)).astype(BF16)
-    f_cross = remote(f_send, f_x, pair_send.at[2], pair_recv.at[2], x_peer)
-    f_cross.start()
-    z_pair.wait_recv()
-
-    def z_sum(x):
-        z_out[block_at(x, kids), :] = (
-            z_own[core, x].astype(F32) + z_core[x].astype(F32)
-        ).astype(BF16)
+    for copy in far_copies[1:]:
+        copy.wait_recv()
+    repeat(groups, child_product)
 
     def z_start(x, n, w):
         remote(
@@ -264,10 +271,8 @@
             z_sem.at[0], z_sem.at[1], (w, n),
         ).start()
 
-    z_sum(1 - along)
     pl.semaphore_wait(ready, 1)
     each_peer(lambda w: z_start(1 - along, x_narrow, w), first=0)
-    z_sum(along)
     each_peer(lambda w: z_start(along, me_n, w))
     mine = block_at(along * wide + me_w, per_peer)
     z_in[mine, :] = z_out[mine, :]
@@ -292,8 +297,9 @@
     out_ref[...] = (total + (added[:, :TILE] + added[:, TILE:])).astype(out_ref.dtype)
 
     messages.wait_send()
+    masks.wait_send()
     arrivals.wait_send()
-    for copy in (f_pair, z_pair, f_cross):
+    for copy in (f_pair, f_cross, *far_copies):
         copy.wait_send()
 
 
@@ -305,22 +311,22 @@
     mask_rows = 16 * pl.cdiv(tile_mask.shape[0], 16)
     shapes = [
         ((rows, cols), BF16),
-        ((kids, touched), BF16),
+        ((2, kids, touched), BF16),
         ((1, kids), jnp.int32),
         (tile_mask.shape, jnp.int32),
         ((2, cols, 2 * TILE), BF16),
         ((mask_rows, TILE), BF16),
+        ((touched, 2 * TILE), BF16),
         ((wide, per_peer + mask_rows, TILE), BF16),
         ((wide, per_peer + mask_rows, TILE), BF16),
-        ((GROUP * per_peer, kids), BF16),
-        ((kids, touched), BF16),
+        ((wide, mask_rows, TILE), BF16),
+        ((kids, kids), BF16),
+        ((kids, 2 * touched), BF16),
         ((rows, kids), BF16),
         ((2, 2, rows, TILE), BF16),
         ((2, rows, TILE), BF16),
         ((rows, TILE), BF16),
         ((rows, TILE), BF16),
-        ((2, 2, kids, TILE), BF16),
-        ((2, kids, TILE), BF16),
         ((2 * kids, TILE), BF16),
         ((2 * kids, TILE), BF16),
     ]
@@ -331,7 +337,7 @@
         in_specs=[pl.BlockSpec(memory_space=pltpu.HBM)] * 5,
         out_specs=pl.BlockSpec(memory_space=pltpu.VMEM),
         scratch_shapes=[pltpu.VMEM(shape, dtype) for shape, dtype in shapes]
-        + [dma((8,)), dma((2,)), dma((2,)), dma((3,)), dma((3,)), pltpu.SemaphoreType.REGULAR],
+        + [dma((8,)), dma((4,)), dma((6,)), dma((2,)), dma((2,)), dma((2,)), pltpu.SemaphoreType.REGULAR],
         compiler_params=pltpu.CompilerParams(
             collective_id=0, has_side_effects=True,
             vmem_limit_bytes=56 * 1024 * 1024,

time: 18.5 us -> 18.5 us (level)
  no operation moved by 1% of the time
where the time goes in v4:
time: 18.5 us; the launch traced here: 18.3 us
  Pallas kernels  17.7 us (96%)
  local copies, waits for them, and re-layouts  0.64 us (3%)
    pallas_call x1, Pallas kernels, local(): pl.pallas_call(functools.partial(kernel, wide, narrow, per_peer, mask_row...  17.7 us
    unnamed x1, local copies, waits for them, and re-layouts  0.64 us

profile of v4, /device:TPU:0, one launch (start us, length us, event | category | flops | bytes accessed | tf_op | source)
XLA Modules:
  0.0 18.3 jit_solution(7296147906467485106)
XLA Ops:
  0.0 17.7 %shard_map.55 = bf16[384,128]{1,0:T(8,128)(2,1)S(1)} custom-call(bf16[384,1280]{1,0:T(8,128)(2,1)} %parent_in.1, bf16[256,512]{1,0:T(8,128)(2,1)} %child_in.1, s32[1,256]{1,0:T(1,128)} %bitcast.1, s32[12,10]{1,0:T(8,128)} %mask_in.1, bf16[1280,512]{1,0:T(8,128)(2,1)} %probes_in.1), custom_call_target="tpu_custom_call" | custom-call | tf_op jit(solution)/shard_map/pallas_call | solution.py:334
  17.7 0.6 %copy.7 = bf16[384,128]{1,0:T(8,128)(2,1)} copy(bf16[384,128]{1,0:T(8,128)(2,1)S(1)} %shard_map.55) | data formatting | bytes 196608

commit v5 on v4

--- a/solution.py
+++ b/solution.py
@@ -67,10 +67,6 @@
     def greet(device):
         pl.semaphore_signal(barrier, inc=1, device_id=device, device_id_type=MESH)
 
-    each_peer(lambda w: greet((w, me_n)))
-    each_peer(lambda w: greet((w, core_narrow)), first=0)
-    greet(x_peer)
-
     pairs = [(map_in, cmap), (mask_in, mask), (child_in, child.at[0]), (parent_in, parent)]
     for n in range(narrow):
         pairs.append(
@@ -82,7 +78,12 @@
     loads = [
         pltpu.make_async_copy(src, dst, load_sem.at[i]) for i, (src, dst) in enumerate(pairs)
     ]
-    for load in loads:
+    for load in loads[:2]:
+        load.start()
+    each_peer(lambda w: greet((w, me_n)))
+    each_peer(lambda w: greet((w, core_narrow)), first=0)
+    greet(x_peer)
+    for load in loads[2:]:
         load.start()
 
     def remote(src, dst, send, recv, device):
@@ -144,6 +145,37 @@
         jnp.broadcast_to(my_mask[None], (GROUP, mask_rows, TILE)),
     ))
 
+    loads[2].wait()
+    repeat(groups, lambda g: sort_group(g, 0))
+
+    part = 384 if rows % 384 == 0 else rows
+
+    def parent_mask(i):
+        at = iota((part, mask_rows), 0) + i * part
+        tile = iota((part, mask_rows), 1) * row_tile
+        spread = jnp.where((at >= tile) & (at < tile + row_tile), 1.0, 0.0).astype(BF16)
+        kept = jnp.dot(spread, my_mask, preferred_element_type=F32).astype(BF16)
+        here = block_at(i, part)
+        for t in range(cols // TILE):
+            span = slice(t * TILE, (t + 1) * TILE)
+            parent[here, span] = parent[here, span] * kept[:, t : t + 1]
+
+    def parent_half(half):
+        def one(i):
+            product = jnp.dot(
+                parent[block_at(i, part), :], probes[half], preferred_element_type=F32
+            ).astype(BF16)
+            for x in range(2):
+                f_own[half, x, block_at(i, part), :] = product[:, x * TILE : (x + 1) * TILE]
+
+        repeat(rows // part, one)
+
+    loads[3].wait()
+    repeat(rows // part, parent_mask)
+    for load in loads[4:]:
+        load.wait()
+    parent_half(1 - core)
+
     pl.semaphore_wait(barrier, 2 * wide)
 
     far_copies = [remote(child_in, child.at[1], far_sem.at[0], far_sem.at[1], core_peer)]
@@ -176,36 +208,6 @@
         msg_sem.at[0], msg_sem.at[1], x_peer,
     )
 
-    loads[2].wait()
-    repeat(groups, lambda g: sort_group(g, 0))
-
-    part = 384 if rows % 384 == 0 else rows
-
-    def parent_mask(i):
-        at = iota((part, mask_rows), 0) + i * part
-        tile = iota((part, mask_rows), 1) * row_tile
-        spread = jnp.where((at >= tile) & (at < tile + row_tile), 1.0, 0.0).astype(BF16)
-        kept = jnp.dot(spread, my_mask, preferred_element_type=F32).astype(BF16)
-        here = block_at(i, part)
-        for t in range(cols // TILE):
-            span = slice(t * TILE, (t + 1) * TILE)
-            parent[here, span] = parent[here, span] * kept[:, t : t + 1]
-
-    def parent_half(half):
-        def one(i):
-            product = jnp.dot(
-                parent[block_at(i, part), :], probes[half], preferred_element_type=F32
-            ).astype(BF16)
-            for x in range(2):
-                f_own[half, x, block_at(i, part), :] = product[:, x * TILE : (x + 1) * TILE]
-
-        repeat(rows // part, one)
-
-    loads[3].wait()
-    repeat(rows // part, parent_mask)
-    for load in loads[4:]:
-        load.wait()
-    parent_half(1 - core)
     f_pair = remote(f_own.at[1 - core], f_core, pair_send.at[0], pair_recv.at[0], core_peer)
     f_pair.start()
     parent_half(core)

time: 18.5 us -> 18.5 us (level)
  no operation moved by 1% of the time
where the time goes in v5:
time: 18.5 us; the launch traced here: 18.3 us
  Pallas kernels  17.7 us (96%)
  local copies, waits for them, and re-layouts  0.64 us (3%)
    pallas_call x1, Pallas kernels, local(): pl.pallas_call(functools.partial(kernel, wide, narrow, per_peer, mask_row...  17.7 us
    unnamed x1, local copies, waits for them, and re-layouts  0.64 us

profile of v5, /device:TPU:0, one launch (start us, length us, event | category | flops | bytes accessed | tf_op | source)
XLA Modules:
  0.0 18.3 jit_solution(14802434701869138537)
XLA Ops:
  0.0 17.7 %shard_map.55 = bf16[384,128]{1,0:T(8,128)(2,1)S(1)} custom-call(bf16[384,1280]{1,0:T(8,128)(2,1)} %parent_in.1, bf16[256,512]{1,0:T(8,128)(2,1)} %child_in.1, s32[1,256]{1,0:T(1,128)} %bitcast.1, s32[12,10]{1,0:T(8,128)} %mask_in.1, bf16[1280,512]{1,0:T(8,128)(2,1)} %probes_in.1), custom_call_target="tpu_custom_call" | custom-call | tf_op jit(solution)/shard_map/pallas_call | solution.py:336
  17.7 0.6 %copy.7 = bf16[384,128]{1,0:T(8,128)(2,1)} copy(bf16[384,128]{1,0:T(8,128)(2,1)S(1)} %shard_map.55) | data formatting | bytes 196608

commit v6 on v5

--- a/solution.py
+++ b/solution.py
@@ -49,15 +49,33 @@
     x_narrow = lax.rem(me_n + 2, narrow)
     x_peer = (me_w, x_narrow)
 
-    def each_peer(fn, first=1):
-        def one(k):
-            fn(lax.rem(me_w + k, wide))
-
+    half_wide = wide // 2
+    my_half = lax.div(me_w, half_wide)
+    my_place = lax.rem(me_w, half_wide)
+
+    def run(first, one):
         if wide <= GROUP:
-            for k in range(first, wide):
+            for k in range(first, half_wide):
                 one(k)
         else:
-            lax.fori_loop(first, wide, lambda k, carry: (one(k), carry)[1], 0)
+            lax.fori_loop(first, half_wide, lambda k, carry: (one(k), carry)[1], 0)
+
+    def each_far(fn):
+        def one(k):
+            place = lax.rem(2 * half_wide - 1 - my_place + k, half_wide)
+            fn((1 - my_half) * half_wide + place)
+
+        run(0, one)
+
+    def each_near(fn, first=1):
+        def one(k):
+            fn(my_half * half_wide + lax.rem(my_place + k, half_wide))
+
+        run(first, one)
+
+    def each_peer(fn):
+        each_far(fn)
+        each_near(fn)
 
     def block_at(index, size):
         return pl.ds(pl.multiple_of(index * size, size), size)
@@ -80,8 +98,12 @@
     ]
     for load in loads[:2]:
         load.start()
-    each_peer(lambda w: greet((w, me_n)))
-    each_peer(lambda w: greet((w, core_narrow)), first=0)
+    def greet_both(w):
+        greet((w, me_n))
+        greet((w, core_narrow))
+
+    each_peer(greet_both)
+    greet(core_peer)
     greet(x_peer)
     for load in loads[2:]:
         load.start()
@@ -177,6 +199,7 @@
     parent_half(1 - core)
 
     pl.semaphore_wait(barrier, 2 * wide)
+    pl.semaphore_signal(ready, inc=1, device_id=x_peer, device_id_type=MESH)
 
     far_copies = [remote(child_in, child.at[1], far_sem.at[0], far_sem.at[1], core_peer)]
     for x in range(2):
@@ -188,19 +211,17 @@
             )
         )
 
-    each_peer(
-        lambda w: remote(
-            msg_out.at[w], msg_in.at[me_w], msg_sem.at[0], msg_sem.at[1], (w, me_n)
-        ).start()
-    )
+    def tell_mask(w):
+        remote(mask_pad, mask_far.at[me_w], msg_sem.at[2], msg_sem.at[3], (w, core_narrow)).start()
+
+    def tell(w):
+        remote(msg_out.at[w], msg_in.at[me_w], msg_sem.at[0], msg_sem.at[1], (w, me_n)).start()
+        tell_mask(w)
+
+    each_peer(tell)
+    tell_mask(me_w)
     for copy in far_copies:
         copy.start()
-    each_peer(
-        lambda w: remote(
-            mask_pad, mask_far.at[me_w], msg_sem.at[2], msg_sem.at[3], (w, core_narrow)
-        ).start(),
-        first=0,
-    )
     msg_in[me_w] = msg_out[me_w]
     masks = remote(mask_far, mask_far, msg_sem.at[2], msg_sem.at[3], core_peer)
     messages = remote(
@@ -252,7 +273,6 @@
 
     def all_in():
         messages.wait_recv()
-        pl.semaphore_signal(ready, inc=1, device_id=x_peer, device_id_type=MESH)
         masks.wait_recv()
 
     if groups == 1:
@@ -274,8 +294,12 @@
         ).start()
 
     pl.semaphore_wait(ready, 1)
-    each_peer(lambda w: z_start(1 - along, x_narrow, w), first=0)
-    each_peer(lambda w: z_start(along, me_n, w))
+    def z_both(w):
+        z_start(1 - along, x_narrow, w)
+        z_start(along, me_n, w)
+
+    each_peer(z_both)
+    z_start(1 - along, x_narrow, me_w)
     mine = block_at(along * wide + me_w, per_peer)
     z_in[mine, :] = z_out[mine, :]
     most = pl.ds(0, (2 * wide - 1) * per_peer)

time: 18.5 us -> 18.5 us (level)
  no operation moved by 1% of the time
where the time goes in v6:
time: 18.5 us; the launch traced here: 18.3 us
  Pallas kernels  17.7 us (96%)
  local copies, waits for them, and re-layouts  0.64 us (3%)
    pallas_call x1, Pallas kernels, local(): pl.pallas_call(functools.partial(kernel, wide, narrow, per_peer, mask_row...  17.7 us
    unnamed x1, local copies, waits for them, and re-layouts  0.64 us

profile of v6, /device:TPU:0, one launch (start us, length us, event | category | flops | bytes accessed | tf_op | source)
XLA Modules:
  0.0 18.3 jit_solution(3394279761566686425)
XLA Ops:
  0.0 17.7 %shard_map.55 = bf16[384,128]{1,0:T(8,128)(2,1)S(1)} custom-call(bf16[384,1280]{1,0:T(8,128)(2,1)} %parent_in.1, bf16[256,512]{1,0:T(8,128)(2,1)} %child_in.1, s32[1,256]{1,0:T(1,128)} %bitcast.1, s32[12,10]{1,0:T(8,128)} %mask_in.1, bf16[1280,512]{1,0:T(8,128)(2,1)} %probes_in.1), custom_call_target="tpu_custom_call" | custom-call | tf_op jit(solution)/shard_map/pallas_call | solution.py:360
  17.7 0.6 %copy.7 = bf16[384,128]{1,0:T(8,128)(2,1)} copy(bf16[384,128]{1,0:T(8,128)(2,1)S(1)} %shard_map.55) | data formatting | bytes 196608

commit v7 on v6

--- a/solution.py
+++ b/solution.py
@@ -211,23 +211,39 @@
             )
         )
 
-    def tell_mask(w):
-        remote(mask_pad, mask_far.at[me_w], msg_sem.at[2], msg_sem.at[3], (w, core_narrow)).start()
-
-    def tell(w):
-        remote(msg_out.at[w], msg_in.at[me_w], msg_sem.at[0], msg_sem.at[1], (w, me_n)).start()
-        tell_mask(w)
-
-    each_peer(tell)
-    tell_mask(me_w)
+    def tell_mask(w, far):
+        remote(
+            mask_pad, mask_far.at[me_w],
+            msg_sem.at[4 * far + 2], msg_sem.at[4 * far + 3], (w, core_narrow),
+        ).start()
+
+    def tell(w, far):
+        remote(
+            msg_out.at[w], msg_in.at[me_w],
+            msg_sem.at[4 * far], msg_sem.at[4 * far + 1], (w, me_n),
+        ).start()
+        tell_mask(w, far)
+
+    each_far(lambda w: tell(w, 1))
+    each_near(lambda w: tell(w, 0))
+    tell_mask(me_w, 0)
     for copy in far_copies:
         copy.start()
     msg_in[me_w] = msg_out[me_w]
-    masks = remote(mask_far, mask_far, msg_sem.at[2], msg_sem.at[3], core_peer)
-    messages = remote(
-        msg_out.at[pl.ds(0, wide - 1)], msg_in.at[pl.ds(0, wide - 1)],
-        msg_sem.at[0], msg_sem.at[1], x_peer,
-    )
+
+    def all_of(buffer_out, buffer_in, count, sems, at):
+        return remote(
+            buffer_out.at[pl.ds(0, count)], buffer_in.at[pl.ds(0, count)],
+            sems.at[at], sems.at[at + 1], x_peer,
+        )
+
+    notices = [
+        (
+            all_of(msg_out, msg_in, half_wide - 1 + far, msg_sem, 4 * far),
+            all_of(mask_far, mask_far, half_wide, msg_sem, 4 * far + 2),
+        )
+        for far in range(2)
+    ]
 
     f_pair = remote(f_own.at[1 - core], f_core, pair_send.at[0], pair_recv.at[0], core_peer)
     f_pair.start()
@@ -237,19 +253,23 @@
 
     shift = mask_rows.bit_length() - 1
 
+    team = GROUP // 2
+    team_slots = team * per_peer
+    teams = half_wide // team
+
     def landing(g):
-        place = msg_out[pl.ds(g * GROUP, GROUP), :per_peer, :].reshape(slots, TILE).astype(F32)
+        place = msg_out[pl.ds(g * team, team), :per_peer, :].reshape(team_slots, TILE).astype(F32)
         place = place[:, 0:1] * 16.0 + place[:, 1:2]
-        lane = iota((slots, GROUP * mask_rows), 1)
-        peer = iota((slots, GROUP * mask_rows), 0) >> (per_peer.bit_length() - 1)
+        lane = iota((team_slots, team * mask_rows), 1)
+        peer = iota((team_slots, team * mask_rows), 0) >> (per_peer.bit_length() - 1)
         tile = ((lane & (mask_rows - 1)) * row_tile).astype(F32)
         same = ((lane >> shift) == peer) & (place >= tile) & (place < tile + row_tile)
         return jnp.where(same, 1.0, 0.0).astype(BF16)
 
     def child_mask(g, tiles):
-        table = msg_in[pl.ds(g * GROUP, GROUP), per_peer:, :].reshape(GROUP * mask_rows, TILE)
-        far = mask_far[pl.ds(g * GROUP, GROUP)].reshape(GROUP * mask_rows, TILE)
-        here = block_at(g, slots)
+        table = msg_in[pl.ds(g * team, team), per_peer:, :].reshape(team * mask_rows, TILE)
+        far = mask_far[pl.ds(g * team, team)].reshape(team * mask_rows, TILE)
+        here = block_at(g, team_slots)
         count = touched // TILE
         for source, part_table in enumerate((table, far)):
             kept = jnp.dot(tiles, part_table, preferred_element_type=F32).astype(BF16)
@@ -258,52 +278,56 @@
                 sorted_rows[here, span] = sorted_rows[here, span] * kept[:, t : t + 1]
 
     def child_product(g):
-        here = block_at(g, slots)
+        here = block_at(g, team_slots)
         product = jnp.dot(
             sorted_rows[here, :touched], probes[core, :touched, :], preferred_element_type=F32
         ) + jnp.dot(sorted_rows[here, touched:], probes_far[...], preferred_element_type=F32)
         product = product.astype(BF16)
         for x in range(2):
-            z_out[block_at(x * groups + g, slots), :] = product[:, x * TILE : (x + 1) * TILE]
+            z_out[block_at(x * 2 * teams + g, team_slots), :] = product[:, x * TILE : (x + 1) * TILE]
 
     f_pair.wait_recv()
     f_send[...] = (f_own[core, 1 - along].astype(F32) + f_core[1 - along].astype(F32)).astype(BF16)
     f_cross = remote(f_send, f_x, pair_send.at[1], pair_recv.at[1], x_peer)
     f_cross.start()
 
-    def all_in():
-        messages.wait_recv()
-        masks.wait_recv()
-
-    if groups == 1:
-        tiles = landing(0)
-        all_in()
-        child_mask(0, tiles)
-    else:
-        all_in()
-        repeat(groups, lambda g: child_mask(g, landing(g)))
-    for copy in far_copies[1:]:
-        copy.wait_recv()
-    repeat(groups, child_product)
-
-    def z_start(x, n, w):
+    def z_start(x, n, w, far):
         remote(
             z_out.at[block_at(x * wide + w, per_peer)],
             z_in.at[block_at(along * wide + me_w, per_peer)],
-            z_sem.at[0], z_sem.at[1], (w, n),
+            z_sem.at[2 * far], z_sem.at[2 * far + 1], (w, n),
         ).start()
 
-    pl.semaphore_wait(ready, 1)
-    def z_both(w):
-        z_start(1 - along, x_narrow, w)
-        z_start(along, me_n, w)
-
-    each_peer(z_both)
-    z_start(1 - along, x_narrow, me_w)
-    mine = block_at(along * wide + me_w, per_peer)
-    z_in[mine, :] = z_out[mine, :]
-    most = pl.ds(0, (2 * wide - 1) * per_peer)
-    arrivals = remote(z_out.at[most], z_in.at[most], z_sem.at[0], z_sem.at[1], x_peer)
+    def z_both(w, far):
+        z_start(1 - along, x_narrow, w, far)
+        z_start(along, me_n, w, far)
+
+    halves = (my_half, 1 - my_half)
+    ahead = [landing(half) for half in halves] if teams == 1 else None
+    for far, half in enumerate(halves):
+        for notice in notices[far]:
+            notice.wait_recv()
+        if teams == 1:
+            child_mask(half, ahead[far])
+        else:
+            repeat(teams, lambda i: child_mask(half * teams + i, landing(half * teams + i)))
+        if far == 0:
+            for copy in far_copies[1:]:
+                copy.wait_recv()
+        repeat(teams, lambda i: child_product(half * teams + i))
+        if far == 0:
+            pl.semaphore_wait(ready, 1)
+            each_near(lambda w: z_both(w, 0))
+            z_start(1 - along, x_narrow, me_w, 0)
+            mine = block_at(along * wide + me_w, per_peer)
+            z_in[mine, :] = z_out[mine, :]
+        else:
+            each_far(lambda w: z_both(w, 1))
+
+    arrivals = [
+        all_of(z_out, z_in, (2 * half_wide - 1 + far) * per_peer, z_sem, 2 * far)
+        for far in range(2)
+    ]
 
     for g in range(groups):
         place = msg_in[g * GROUP : (g + 1) * GROUP, :per_peer, :].reshape(slots, TILE)
@@ -317,14 +341,18 @@
         ).astype(BF16)
     f_cross.wait_recv()
     total = f_own[core, along].astype(F32) + f_core[along].astype(F32) + f_x[...].astype(F32)
-    arrivals.wait_recv()
-    both_chips = jnp.concatenate([z_in[:kids, :], z_in[kids:, :]], axis=1)
-    added = jnp.dot(lands[...], both_chips, preferred_element_type=F32)
-    out_ref[...] = (total + (added[:, :TILE] + added[:, TILE:])).astype(out_ref.dtype)
-
-    messages.wait_send()
-    masks.wait_send()
-    arrivals.wait_send()
+    for far, half in enumerate(halves):
+        arrivals[far].wait_recv()
+        size = kids // 2
+        both_chips = jnp.concatenate(
+            [z_in[block_at(half, size), :], z_in[block_at(2 + half, size), :]], axis=1
+        )
+        added = jnp.dot(lands[:, block_at(half, size)], both_chips, preferred_element_type=F32)
+        total = total + (added[:, :TILE] + added[:, TILE:])
+    out_ref[...] = total.astype(out_ref.dtype)
+
+    for copy in (*notices[0], *notices[1], *arrivals):
+        copy.wait_send()
     for copy in (f_pair, f_cross, *far_copies):
         copy.wait_send()
 
@@ -363,7 +391,7 @@
         in_specs=[pl.BlockSpec(memory_space=pltpu.HBM)] * 5,
         out_specs=pl.BlockSpec(memory_space=pltpu.VMEM),
         scratch_shapes=[pltpu.VMEM(shape, dtype) for shape, dtype in shapes]
-        + [dma((8,)), dma((4,)), dma((6,)), dma((2,)), dma((2,)), dma((2,)), pltpu.SemaphoreType.REGULAR],
+        + [dma((8,)), dma((8,)), dma((6,)), dma((4,)), dma((2,)), dma((2,)), pltpu.SemaphoreType.REGULAR],
         compiler_params=pltpu.CompilerParams(
             collective_id=0, has_side_effects=True,
             vmem_limit_bytes=56 * 1024 * 1024,

time: 18.5 us -> 18.7 us (1.011)
  Pallas kernels: 17.7 us -> 17.9 us
    pallas_call x1, Pallas kernels: 17.7 us -> 17.9 us  [local(): pl.pallas_call(functools.partial(kernel, wide, narrow, per_peer, mask_row...]
where the time goes in v7:
time: 18.7 us; the launch traced here: 18.6 us
  Pallas kernels  17.9 us (96%)
  local copies, waits for them, and re-layouts  0.64 us (3%)
    pallas_call x1, Pallas kernels, local(): pl.pallas_call(functools.partial(kernel, wide, narrow, per_peer, mask_row...  17.9 us
    unnamed x1, local copies, waits for them, and re-layouts  0.64 us

profile of v7, /device:TPU:0, one launch (start us, length us, event | category | flops | bytes accessed | tf_op | source)
XLA Modules:
  0.0 18.6 jit_solution(2188769353744883215)
XLA Ops:
  0.0 17.9 %shard_map.55 = bf16[384,128]{1,0:T(8,128)(2,1)S(1)} custom-call(bf16[384,1280]{1,0:T(8,128)(2,1)} %parent_in.1, bf16[256,512]{1,0:T(8,128)(2,1)} %child_in.1, s32[1,256]{1,0:T(1,128)} %bitcast.1, s32[12,10]{1,0:T(8,128)} %mask_in.1, bf16[1280,512]{1,0:T(8,128)(2,1)} %probes_in.1), custom_call_target="tpu_custom_call" | custom-call | tf_op jit(solution)/shard_map/pallas_call | solution.py:388
  17.9 0.6 %copy.7 = bf16[384,128]{1,0:T(8,128)(2,1)} copy(bf16[384,128]{1,0:T(8,128)(2,1)S(1)} %shard_map.55) | data formatting | bytes 196608

commit v8 on v6

--- a/solution.py
+++ b/solution.py
@@ -32,7 +32,7 @@
     parent, child, cmap, mask, probes, mask_pad,
     probes_far, msg_out, msg_in, mask_far, pick, sorted_rows, lands,
     f_own, f_core, f_send, f_x,
-    z_out, z_in,
+    z_out, z_in, tile_products, keep,
     load_sem, msg_sem, far_sem, z_sem, pair_send, pair_recv, ready,
 ):
     rows, cols = parent.shape
@@ -62,8 +62,7 @@
 
     def each_far(fn):
         def one(k):
-            place = lax.rem(2 * half_wide - 1 - my_place + k, half_wide)
-            fn((1 - my_half) * half_wide + place)
+            fn((1 - my_half) * (wide - 1 - k) + my_half * k)
 
         run(0, one)
 
@@ -96,8 +95,6 @@
     loads = [
         pltpu.make_async_copy(src, dst, load_sem.at[i]) for i, (src, dst) in enumerate(pairs)
     ]
-    for load in loads[:2]:
-        load.start()
     def greet_both(w):
         greet((w, me_n))
         greet((w, core_narrow))
@@ -105,7 +102,7 @@
     each_peer(greet_both)
     greet(core_peer)
     greet(x_peer)
-    for load in loads[2:]:
+    for load in loads:
         load.start()
 
     def remote(src, dst, send, recv, device):
@@ -275,17 +272,6 @@
         messages.wait_recv()
         masks.wait_recv()
 
-    if groups == 1:
-        tiles = landing(0)
-        all_in()
-        child_mask(0, tiles)
-    else:
-        all_in()
-        repeat(groups, lambda g: child_mask(g, landing(g)))
-    for copy in far_copies[1:]:
-        copy.wait_recv()
-    repeat(groups, child_product)
-
     def z_start(x, n, w):
         remote(
             z_out.at[block_at(x * wide + w, per_peer)],
@@ -293,12 +279,48 @@
             z_sem.at[0], z_sem.at[1], (w, n),
         ).start()
 
-    pl.semaphore_wait(ready, 1)
     def z_both(w):
         z_start(1 - along, x_narrow, w)
         z_start(along, me_n, w)
 
-    each_peer(z_both)
+    if groups == 1:
+        count = touched // TILE
+        tiles = landing(0)
+        for copy in far_copies[1:]:
+            copy.wait_recv()
+        for t in range(2 * count):
+            span = slice(t % count * TILE, (t % count + 1) * TILE)
+            weights = probes_far[span, :] if t >= count else probes[core, span, :]
+            tile_products[t] = jnp.dot(
+                sorted_rows[:, t * TILE : (t + 1) * TILE], weights, preferred_element_type=F32
+            )
+        all_in()
+        pl.semaphore_wait(ready, 1)
+        kept = [
+            jnp.dot(tiles, table.reshape(GROUP * mask_rows, TILE), preferred_element_type=F32)
+            for table in (msg_in[:, per_peer:, :], mask_far[...])
+        ]
+        keep[0] = kept[0]
+        keep[1] = kept[1]
+        size = kids // 2
+        for half, each in ((1 - my_half, each_far), (my_half, each_near)):
+            here = block_at(half, size)
+            product = jnp.zeros((size, 2 * TILE), F32)
+            for t in range(2 * count):
+                factor = keep[t // count, here, t % count : t % count + 1]
+                product = product + factor * tile_products[t, here, :]
+            product = product.astype(BF16)
+            for x in range(2):
+                z_out[block_at(x * 2 + half, size), :] = product[:, x * TILE : (x + 1) * TILE]
+            each(z_both)
+    else:
+        all_in()
+        repeat(groups, lambda g: child_mask(g, landing(g)))
+        for copy in far_copies[1:]:
+            copy.wait_recv()
+        repeat(groups, child_product)
+        pl.semaphore_wait(ready, 1)
+        each_peer(z_both)
     z_start(1 - along, x_narrow, me_w)
     mine = block_at(along * wide + me_w, per_peer)
     z_in[mine, :] = z_out[mine, :]
@@ -355,6 +377,8 @@
         ((rows, TILE), BF16),
         ((2 * kids, TILE), BF16),
         ((2 * kids, TILE), BF16),
+        ((2 * touched // TILE, GROUP * per_peer, 2 * TILE), F32),
+        ((2, GROUP * per_peer, TILE), F32),
     ]
     dma = pltpu.SemaphoreType.DMA
     return pl.pallas_call(

time: 18.5 us -> 17.4 us (0.941)
  Pallas kernels: 17.7 us -> 16.6 us
    pallas_call x1, Pallas kernels: 17.7 us -> 16.6 us  [local(): pl.pallas_call(functools.partial(kernel, wide, narrow, per_peer, mask_row...]
where the time goes in v8:
time: 17.4 us; the launch traced here: 17.2 us
  Pallas kernels  16.6 us (95%)
  local copies, waits for them, and re-layouts  0.64 us (4%)
    pallas_call x1, Pallas kernels, local(): pl.pallas_call(functools.partial(kernel, wide, narrow, per_peer, mask_row...  16.6 us
    unnamed x1, local copies, waits for them, and re-layouts  0.64 us

profile of v8, /device:TPU:0, one launch (start us, length us, event | category | flops | bytes accessed | tf_op | source)
XLA Modules:
  0.0 17.2 jit_solution(494273063548462177)
XLA Ops:
  0.0 16.6 %shard_map.55 = bf16[384,128]{1,0:T(8,128)(2,1)S(1)} custom-call(bf16[384,1280]{1,0:T(8,128)(2,1)} %parent_in.1, bf16[256,512]{1,0:T(8,128)(2,1)} %child_in.1, s32[1,256]{1,0:T(1,128)} %bitcast.1, s32[12,10]{1,0:T(8,128)} %mask_in.1, bf16[1280,512]{1,0:T(8,128)(2,1)} %probes_in.1), custom_call_target="tpu_custom_call" | custom-call | tf_op jit(solution)/shard_map/pallas_call | solution.py:384
  16.6 0.6 %copy.7 = bf16[384,128]{1,0:T(8,128)(2,1)} copy(bf16[384,128]{1,0:T(8,128)(2,1)S(1)} %shard_map.55) | data formatting | bytes 196608

commit v9 on v8

--- a/solution.py
+++ b/solution.py
@@ -302,17 +302,27 @@
         ]
         keep[0] = kept[0]
         keep[1] = kept[1]
-        size = kids // 2
-        for half, each in ((1 - my_half, each_far), (my_half, each_near)):
-            here = block_at(half, size)
-            product = jnp.zeros((size, 2 * TILE), F32)
+
+        def z_block(w):
+            here = block_at(w, per_peer)
+            product = jnp.zeros((per_peer, 2 * TILE), F32)
             for t in range(2 * count):
                 factor = keep[t // count, here, t % count : t % count + 1]
                 product = product + factor * tile_products[t, here, :]
             product = product.astype(BF16)
             for x in range(2):
-                z_out[block_at(x * 2 + half, size), :] = product[:, x * TILE : (x + 1) * TILE]
-            each(z_both)
+                z_out[block_at(x * wide + w, per_peer), :] = product[:, x * TILE : (x + 1) * TILE]
+
+        def z_blocks(w):
+            z_block(w)
+            z_start(core, 3 * core, w)
+            z_start(1 - core, 2 - core, w)
+
+        for k in range(half_wide):
+            low = k + core * (half_wide - 1 - 2 * k)
+            z_blocks((1 - my_half) * (wide - 1 - k) + my_half * low)
+        each_near(z_blocks)
+        z_block(me_w)
     else:
         all_in()
         repeat(groups, lambda g: child_mask(g, landing(g)))

time: 17.4 us -> 17.8 us (1.023)
  the two profiles are of different devices: /device:TPU:0 before, /device:TPU:1 now
where the time goes in v9:
time: 17.8 us; the launch traced here: 17.6 us
  Pallas kernels  16.9 us (95%)
  local copies, waits for them, and re-layouts  0.64 us (4%)
    pallas_call x1, Pallas kernels, local(): pl.pallas_call(functools.partial(kernel, wide, narrow, per_peer, mask_row...  16.9 us
    unnamed x1, local copies, waits for them, and re-layouts  0.64 us

profile of v9, /device:TPU:1, one launch (start us, length us, event | category | flops | bytes accessed | tf_op | source)
XLA Modules:
  0.0 17.6 jit_solution(569656252461759085)
XLA Ops:
  0.0 16.9 %shard_map.55 = bf16[384,128]{1,0:T(8,128)(2,1)S(1)} custom-call(bf16[384,1280]{1,0:T(8,128)(2,1)} %parent_in.1, bf16[256,512]{1,0:T(8,128)(2,1)} %child_in.1, s32[1,256]{1,0:T(1,128)} %bitcast.1, s32[12,10]{1,0:T(8,128)} %mask_in.1, bf16[1280,512]{1,0:T(8,128)(2,1)} %probes_in.1), custom_call_target="tpu_custom_call" | custom-call | tf_op jit(solution)/shard_map/pallas_call | solution.py:394
  17.0 0.6 %copy.7 = bf16[384,128]{1,0:T(8,128)(2,1)} copy(bf16[384,128]{1,0:T(8,128)(2,1)S(1)} %shard_map.55) | data formatting | bytes 196608

commit v10 on v9

--- a/solution.py
+++ b/solution.py
@@ -315,12 +315,10 @@
 
         def z_blocks(w):
             z_block(w)
-            z_start(core, 3 * core, w)
-            z_start(1 - core, 2 - core, w)
-
-        for k in range(half_wide):
-            low = k + core * (half_wide - 1 - 2 * k)
-            z_blocks((1 - my_half) * (wide - 1 - k) + my_half * low)
+            z_start(0, core, w)
+            z_start(1, 2 + core, w)
+
+        each_far(z_blocks)
         each_near(z_blocks)
         z_block(me_w)
     else:

time: 17.8 us -> 17.3 us (0.972)
  the two profiles are of different devices: /device:TPU:1 before, /device:TPU:0 now
where the time goes in v10:
time: 17.3 us; the launch traced here: 17.1 us
  Pallas kernels  16.5 us (95%)
  local copies, waits for them, and re-layouts  0.64 us (4%)
    pallas_call x1, Pallas kernels, local(): pl.pallas_call(functools.partial(kernel, wide, narrow, per_peer, mask_row...  16.5 us
    unnamed x1, local copies, waits for them, and re-layouts  0.64 us

profile of v10, /device:TPU:0, one launch (start us, length us, event | category | flops | bytes accessed | tf_op | source)
XLA Modules:
  0.0 17.1 jit_solution(8392795478031407249)
XLA Ops:
  0.0 16.5 %shard_map.55 = bf16[384,128]{1,0:T(8,128)(2,1)S(1)} custom-call(bf16[384,1280]{1,0:T(8,128)(2,1)} %parent_in.1, bf16[256,512]{1,0:T(8,128)(2,1)} %child_in.1, s32[1,256]{1,0:T(1,128)} %bitcast.1, s32[12,10]{1,0:T(8,128)} %mask_in.1, bf16[1280,512]{1,0:T(8,128)(2,1)} %probes_in.1), custom_call_target="tpu_custom_call" | custom-call | tf_op jit(solution)/shard_map/pallas_call | solution.py:392
  16.5 0.6 %copy.7 = bf16[384,128]{1,0:T(8,128)(2,1)} copy(bf16[384,128]{1,0:T(8,128)(2,1)S(1)} %shard_map.55) | data formatting | bytes 196608

commit v11 on v10

--- a/solution.py
+++ b/solution.py
@@ -263,10 +263,12 @@
         for x in range(2):
             z_out[block_at(x * groups + g, slots), :] = product[:, x * TILE : (x + 1) * TILE]
 
-    f_pair.wait_recv()
-    f_send[...] = (f_own[core, 1 - along].astype(F32) + f_core[1 - along].astype(F32)).astype(BF16)
     f_cross = remote(f_send, f_x, pair_send.at[1], pair_recv.at[1], x_peer)
-    f_cross.start()
+
+    def send_parent():
+        f_pair.wait_recv()
+        f_send[...] = (f_own[core, 1 - along].astype(F32) + f_core[1 - along].astype(F32)).astype(BF16)
+        f_cross.start()
 
     def all_in():
         messages.wait_recv()
@@ -294,6 +296,7 @@
             tile_products[t] = jnp.dot(
                 sorted_rows[:, t * TILE : (t + 1) * TILE], weights, preferred_element_type=F32
             )
+        send_parent()
         all_in()
         pl.semaphore_wait(ready, 1)
         kept = [
@@ -322,6 +325,7 @@
         each_near(z_blocks)
         z_block(me_w)
     else:
+        send_parent()
         all_in()
         repeat(groups, lambda g: child_mask(g, landing(g)))
         for copy in far_copies[1:]:

time: 17.3 us -> 17.3 us (level)
  no operation moved by 1% of the time
where the time goes in v11:
time: 17.3 us; the launch traced here: 17.1 us
  Pallas kernels  16.5 us (95%)
  local copies, waits for them, and re-layouts  0.64 us (4%)
    pallas_call x1, Pallas kernels, local(): pl.pallas_call(functools.partial(kernel, wide, narrow, per_peer, mask_row...  16.5 us
    unnamed x1, local copies, waits for them, and re-layouts  0.64 us

profile of v11, /device:TPU:0, one launch (start us, length us, event | category | flops | bytes accessed | tf_op | source)
XLA Modules:
  0.0 17.1 jit_solution(3443252085247037337)
XLA Ops:
  0.0 16.5 %shard_map.55 = bf16[384,128]{1,0:T(8,128)(2,1)S(1)} custom-call(bf16[384,1280]{1,0:T(8,128)(2,1)} %parent_in.1, bf16[256,512]{1,0:T(8,128)(2,1)} %child_in.1, s32[1,256]{1,0:T(1,128)} %bitcast.1, s32[12,10]{1,0:T(8,128)} %mask_in.1, bf16[1280,512]{1,0:T(8,128)(2,1)} %probes_in.1), custom_call_target="tpu_custom_call" | custom-call | tf_op jit(solution)/shard_map/pallas_call | solution.py:396
  16.5 0.6 %copy.7 = bf16[384,128]{1,0:T(8,128)(2,1)} copy(bf16[384,128]{1,0:T(8,128)(2,1)S(1)} %shard_map.55) | data formatting | bytes 196608
